TPU v7x, 256 devices: a whole 4x4x8 slice. The times are simulated.
256 devices in a mesh: wide: 32 (over y, x, core), lon: 8 (over z).
Axes of the slice: x: 4, y: 4, z: 8, core: 2. Of those that a mesh axis runs over, the one named last changes fastest.
Arguments:
- background_ensemble: bfloat16 [256, 256, 2048], P('wide', None, 'lon'), may hold values from -6 to 6
- innov: bfloat16 [256, 256, 2048], P(None, 'wide', 'lon'), may hold values from -6 to 6
- obs_index: int32 [4, 256, 2048], P(None, None, 'lon'), may hold values from 0 to 65535, as said below
- obs_weight: float32 [4, 256, 2048], P(None, None, 'lon'), may hold values from 0.05 to 0.5
- obs_list: int32 [8, 512, 16], P('lon', 'wide'), may hold values from 0 to 23, as said below
- tile_count: int32 [8, 512], P('lon', 'wide'), may hold values from 1 to 16
- taper_class: int32 [8, 512, 16], P('lon', 'wide'), may hold values from 0 to 3
Outputs:
- analysis: bfloat16 [256, 256, 2048], P('wide', None, 'lon')
Inputs may be any that keep to these rules, and one draw needn't show every extreme that they name: obs_index[k, i, c] = r * 256 + q names the cell in row r and column q of the observation's own longitude tile, and row r lies among the 8 rows of the region that holds row i. Each row of obs_list names 16 different candidates of its region.
All inputs are finite; a program needn't handle non-finite values.
Results may differ from a plain program's by a relative error of at most 0.0056.
Values may be sent and summed in bfloat16 or wider, within the bound.
A program may use at most 64 MiB of HBM per device.

v0:
```python
import math

import jax
import jax.numpy as jnp
from jax import lax
from jax.sharding import PartitionSpec as P

BLK = 128
HALO_BLK = 4


def padded_2(value, sides, width):
    for axis, dim in sides:
        size, length = (lax.axis_size(axis), value.shape[dim])
        up = [(i, (i + 1) % size) for i in range(size)]
        down = [(j, i) for i, j in up]
        last = lax.slice_in_dim(value, length - width, length, axis=dim)
        first = lax.slice_in_dim(value, 0, width, axis=dim)
        before = lax.ppermute(last, axis, up)
        after = lax.ppermute(first, axis, down)
        value = jnp.concatenate([before, value, after], axis=dim)
    return value


def observe_region(state, index, weight):
    members, cells = state.shape
    width = math.gcd(512, cells)
    nblocks = cells // width
    index_blocks = index.reshape(4, nblocks, width).transpose(1, 0, 2)
    weight_blocks = weight.reshape(4, nblocks, width).transpose(1, 0, 2)
    cell_ids = lax.broadcasted_iota(jnp.int32, (cells, width), 0)

    def observe_one_block(pieces):
        index_here, weight_here = pieces
        summed = jnp.zeros((members, width), jnp.float32)
        for k in range(4):
            selector = (cell_ids == index_here[k][None, :]).astype(jnp.bfloat16)
            picked = jnp.dot(state, selector, preferred_element_type=jnp.float32)
            summed = summed + weight_here[k][None, :] * picked
        return summed.astype(jnp.bfloat16)

    result = lax.map(observe_one_block, (index_blocks, weight_blocks))
    return result.transpose(1, 0, 2).reshape(members, cells)


def anomaly_from_mean(state_values):
    centred = state_values.astype(jnp.float32)
    return (centred - jnp.mean(centred, axis=-2, keepdims=True)).astype(jnp.bfloat16)


def taper_tiles(classes, in_use, tile_width):
    row_ids = lax.broadcasted_iota(jnp.float32, (tile_width, tile_width), 0)
    col_ids = lax.broadcasted_iota(jnp.float32, (tile_width, tile_width), 1)
    offset = row_ids - col_ids
    length = 8.0 * jnp.exp2(classes.astype(jnp.float32))
    scaled = offset / length[..., None, None]
    return in_use[..., None, None] / (1.0 + scaled * scaled)


def body(background_ensemble, innov, obs_index, obs_weight, obs_list, tile_count, taper_class):
    padded = padded_2(background_ensemble, (("lon", 2),), 1)
    state_values = background_ensemble.astype(jnp.float32)
    east_neighbour = padded[:, :, 2:].astype(jnp.float32)
    west_neighbour = padded[:, :, :-2].astype(jnp.float32)
    northern = jnp.pad(state_values[:, 1:, :], ((0, 0), (0, 1), (0, 0)))
    southern = jnp.pad(state_values[:, :-1, :], ((0, 0), (1, 0), (0, 0)))
    member_spread = east_neighbour + west_neighbour + northern + southern - 4.0 * state_values
    prediction_increment = (
        state_values + 0.2 * member_spread - 0.3 * (east_neighbour - west_neighbour)
    ).astype(jnp.bfloat16)
    ensemble_lines_here, whole_parallel_set, patch_meridian_lines = prediction_increment.shape
    members = innov.shape[0]
    band_rows = innov.shape[1]
    patch_gridpoints = band_rows * patch_meridian_lines
    region = lax.all_to_all(prediction_increment, "wide", split_axis=1, concat_axis=0, tiled=True)
    region_state = region.reshape(members, patch_gridpoints)
    first_row = lax.axis_index("wide") * band_rows
    local_index = lax.dynamic_slice_in_dim(obs_index, first_row, band_rows, 1).reshape(
        4, patch_gridpoints
    )
    local_index = local_index - first_row * patch_meridian_lines
    local_weight = lax.dynamic_slice_in_dim(obs_weight, first_row, band_rows, 1).reshape(
        4, patch_gridpoints
    )
    region_obs = observe_region(region_state, local_index, local_weight)
    model_anomaly = anomaly_from_mean(region_state)
    obs_dev = anomaly_from_mean(region_obs)
    stacked = jnp.stack([obs_dev, innov.reshape(members, patch_gridpoints)])
    widened = padded_2(stacked, (("lon", 2),), HALO_BLK * BLK)
    candidate_count = widened.shape[2] // BLK
    cand = widened.reshape(2, members, candidate_count, BLK)
    block_count = patch_gridpoints // BLK
    candidate_ids = lax.broadcasted_iota(jnp.int32, (obs_list.shape[2], candidate_count), 1)

    def body_one_block(position, result):
        start = position * BLK
        state_tile = lax.dynamic_slice_in_dim(model_anomaly, start, BLK, 1)
        anchor = lax.dynamic_slice_in_dim(region_state, start, BLK, 1)
        listed = obs_list[0, position]
        classes = taper_class[0, position]
        live_count = tile_count[0, position]
        selector = (candidate_ids == listed[:, None]).astype(jnp.bfloat16)
        picked = jnp.einsum(
            "jk,smko->smjo", selector, cand, preferred_element_type=jnp.float32
        ).astype(jnp.bfloat16)
        covariance = jnp.einsum(
            "mc,mjo->jco", state_tile, picked[0], preferred_element_type=jnp.float32
        ) / (members - 1.0)
        in_use = (jnp.arange(listed.shape[0], dtype=jnp.int32) < live_count).astype(jnp.float32)
        tapered = (covariance * taper_tiles(classes, in_use, BLK)).astype(jnp.bfloat16)
        change = jnp.einsum("mjo,jco->mc", picked[1], tapered, preferred_element_type=jnp.float32)
        updated = (anchor.astype(jnp.float32) + change).astype(jnp.bfloat16)
        return lax.dynamic_update_slice_in_dim(result, updated, start, 1)

    result = lax.fori_loop(
        0, block_count, body_one_block, jnp.zeros((members, patch_gridpoints), jnp.bfloat16)
    )
    return lax.all_to_all(
        result.reshape(members, band_rows, patch_meridian_lines),
        "wide",
        split_axis=0,
        concat_axis=1,
        tiled=True,
    )


def solution(mesh):
    in_specs = (
        P("wide", None, "lon"),
        P(None, "wide", "lon"),
        P(None, None, "lon"),
        P(None, None, "lon"),
        P("lon", "wide", None),
        P("lon", "wide"),
        P("lon", "wide", None),
    )
    out_specs = P("wide", None, "lon")
    return jax.shard_map(body, mesh=mesh, in_specs=in_specs, out_specs=out_specs, check_vma=False)
```

profile of v0, /device:TPU:1, one launch (start us, length us, event | category | flops | bytes accessed | tf_op | source)
XLA Modules:
  0.0 263.4 jit_solution(12337701517257284341)
XLA Ops:
  0.0 2.0 fusion.95
  2.2 6.5 %collective-permute-start = (bf16[8,256,1]{2,0,1:T(8,128)(2,1)S(1)}, bf16[8,256,1]{2,0,1:T(8,128)(2,1)S(1)}, u32[]{:S(2)}, u32[]{:S(2)}) collective-permute-start(bf16[8,256,1]{2,0,1:T(8,128)(2,1)S(1)} %get-tuple-element.305), channel_id=1, source_target_pairs={{1,0},{2,1},{3,2},{4,3},{5,4},{6,5},{7,6},{0,7},{9,8},{10,9},{11,1... | collective-permute-start | bytes 12296 | tf_op jit(solution)/shard_map/ppermute | solution.py:20
  9.0 10.3 %collective-permute-done = bf16[8,256,1]{2,0,1:T(8,128)(2,1)S(1)} collective-permute-done((bf16[8,256,1]{2,0,1:T(8,128)(2,1)S(1)}, bf16[8,256,1]{2,0,1:T(8,128)(2,1)S(1)}, u32[]{:S(2)}, u32[]{:S(2)}) %collective-permute-start) | collective-permute-done | bytes 4128 | tf_op jit(solution)/shard_map/ppermute | solution.py:20
  19.3 3.1 %collective-permute-done.1 = bf16[8,256,1]{2,0,1:T(8,128)(2,1)S(1)} collective-permute-done((bf16[8,256,1]{2,0,1:T(8,128)(2,1)S(1)}, bf16[8,256,1]{2,0,1:T(8,128)(2,1)S(1)}, u32[]{:S(2)}, u32[]{:S(2)}) %collective-permute-start.1) | collective-permute-done | bytes 4128 | tf_op jit(solution)/shard_map/ppermute | solution.py:19
  22.4 2.7 %fusion.90 = bf16[8,256,256]{2,0,1:T(8,128)(2,1)} fusion(f32[8,255,256]{2,0,1:T(8,128)S(1)} %get-tuple-element.304, f32[8,255,256]{2,0,1:T(8,128)S(1)} %get-tuple-element.303, bf16[8,256,256]{2,0,1:T(8,128)(2,1)S(1)} %get-tuple-element.307, bf16[8,256,1]{2,0,1:T(8,128)(2,1)S(1)} %collective-permute-done.1, bf16[8,256,1]{2,0,1:T(8,128)(2,1)S(1)} %collective-permute-done), kind=kLoop, calls=%fused_computation.85 | loop fusion | flops 10485760 | bytes 6283264 | tf_op jit(solution)/shard_map/convert_element_type | solution.py:70
  25.1 9.0 %all-to-all-start = ((bf16[8,256,256]{2,0,1:T(8,128)(2,1)}), bf16[8,256,256]{2,0,1:T(8,128)(2,1)}, u32[]{:S(2)}, u32[]{:S(2)}) async-start(bf16[8,256,256]{2,0,1:T(8,128)(2,1)} %fusion.90), calls=%async_computation | async-start | bytes 2097152 | tf_op jit(solution)/shard_map/all_to_all | solution.py:75
  35.0 1.6 copy.42
  36.6 14.7 %all-to-all-done = bf16[8,256,256]{2,0,1:T(8,128)(2,1)} async-done(((bf16[8,256,256]{2,0,1:T(8,128)(2,1)}), bf16[8,256,256]{2,0,1:T(8,128)(2,1)}, u32[]{:S(2)}, u32[]{:S(2)}) %all-to-all-start) | async-done | bytes 1048608 | tf_op jit(solution)/shard_map/all_to_all | solution.py:75
  51.4 32.1 %while.27 = (s32[]{:T(128)}, bf16[4,256,512]{1,2,0:T(8,128)(2,1)S(1)}, f32[4,4,512]{2,0,1:T(4,128)S(1)}, s32[4,4,512]{2,0,1:T(4,128)S(1)}, bf16[256,2048]{1,0:T(...) while((s32[]{:T(128)}, bf16[4,256,512]{1,2,0:T(8,128)(2,1)S(1)}, ...), condition=%wide.region_2.3_spmd.clone.clone, body=%wide.region_1.2_spmd.clone.clone.sunk | while | flops 2156920832 | bytes 7651501 | solution.py:42
  51.4 2.0 fusion.135
  53.4 2.0 fusion.136
  55.4 2.0 fusion.137
  57.4 2.0 fusion.138
  59.4 2.0 fusion.135
  61.4 2.0 fusion.136
  63.4 2.0 fusion.137
  65.4 2.0 fusion.138
  67.5 2.0 fusion.135
  69.5 2.0 fusion.136
  71.4 2.0 fusion.137
  73.4 2.0 fusion.138
  75.5 2.0 fusion.135
  77.5 2.0 fusion.136
  79.5 2.0 fusion.137
  81.5 2.0 fusion.138
  84.6 2.7 %collective-permute-start.3 = (bf16[2,256,512]{1,2,0:T(8,128)(2,1)S(1)}, bf16[2,256,512]{1,2,0:T(8,128)(2,1)S(1)}, u32[]{:S(2)}, u32[]{:S(2)}) collective-permute-start(bf16[2,256,512]{1,2,0:T(8,128)(2,1)S(1)} %get-tuple-element.302), channel_id=1, source_target_pairs={{1,0},{2,1},{3,2},{4,3},{5,4},{6,5},{7,6},{0,7},{9,8},{10,9},{11,1... | collective-permute-start | bytes 1572872 | tf_op jit(solution)/shard_map/ppermute | solution.py:20
  88.6 2.5 subtract_convert_fusion
  91.1 7.8 %collective-permute-done.2 = bf16[2,256,512]{1,2,0:T(8,128)(2,1)S(1)} collective-permute-done((bf16[2,256,512]{1,2,0:T(8,128)(2,1)S(1)}, bf16[2,256,512]{1,2,0:T(8,128)(2,1)S(1)}, u32[]{:S(2)}, u32[]{:S(2)}) %collective-permute-start.2) | collective-permute-done | bytes 524320 | tf_op jit(solution)/shard_map/ppermute | solution.py:19
  98.9 1.8 pad_maximum_fusion
  100.7 4.8 %copy.43 = bf16[2,256,24,128]{3,2,1,0:T(8,128)(2,1)} copy(bf16[2,256,24,128]{1,3,2,0:T(8,128)(2,1)} %bitcast.155) | data formatting | bytes 6291456 | tf_op jit(solution)/shard_map/reshape | solution.py:91
  106.6 132.7 %while.26 = (s32[]{:T(128)}, bf16[256,2048]{1,0:T(8,128)(2,1)}, bf16[256,2048]{1,0:T(8,128)(2,1)}, s32[1,16,16]{2,1,0:T(8,128)}, bf16[2,256,24,128]{3,2,1,0:T(8,...) while((s32[]{:T(128)}, bf16[256,2048]{1,0:T(8,128)(2,1)}, ...), condition=%wide.region_5.6_spmd.clone, body=%wide.region_4.5_spmd.clone.sunk | while | flops 321765856 | bytes 11863739 | solution.py:115
  107.3 2.7 %convert_bitcast_fusion.2 = bf16[2,256,16,128]{3,2,1,0:T(8,128)(2,1)S(1)} fusion(bf16[2,256,24,128]{3,2,1,0:T(8,128)(2,1)} %get-tuple-element.467, s32[16]{0:T(128)S(1)} %fusion.125), kind=kOutput, calls=%fused_computation.2.clone.1 | convolution fusion | flops 51380608 | bytes 5242944 | tf_op jit(solution)/shard_map/while/body/eval_jaxpr/jk,smko->smjo/dot_general | solution.py:103
  112.4 2.5 fusion.126
  115.6 2.7 %convert_bitcast_fusion.2 = bf16[2,256,16,128]{3,2,1,0:T(8,128)(2,1)S(1)} fusion(bf16[2,256,24,128]{3,2,1,0:T(8,128)(2,1)} %get-tuple-element.467, s32[16]{0:T(128)S(1)} %fusion.125), kind=kOutput, calls=%fused_computation.2.clone.1 | convolution fusion | flops 51380608 | bytes 5242944 | tf_op jit(solution)/shard_map/while/body/eval_jaxpr/jk,smko->smjo/dot_general | solution.py:103
  120.7 2.5 fusion.126
  123.9 2.7 %convert_bitcast_fusion.2 = bf16[2,256,16,128]{3,2,1,0:T(8,128)(2,1)S(1)} fusion(bf16[2,256,24,128]{3,2,1,0:T(8,128)(2,1)} %get-tuple-element.467, s32[16]{0:T(128)S(1)} %fusion.125), kind=kOutput, calls=%fused_computation.2.clone.1 | convolution fusion | flops 51380608 | bytes 5242944 | tf_op jit(solution)/shard_map/while/body/eval_jaxpr/jk,smko->smjo/dot_general | solution.py:103
  129.0 2.5 fusion.126
  132.2 2.7 %convert_bitcast_fusion.2 = bf16[2,256,16,128]{3,2,1,0:T(8,128)(2,1)S(1)} fusion(bf16[2,256,24,128]{3,2,1,0:T(8,128)(2,1)} %get-tuple-element.467, s32[16]{0:T(128)S(1)} %fusion.125), kind=kOutput, calls=%fused_computation.2.clone.1 | convolution fusion | flops 51380608 | bytes 5242944 | tf_op jit(solution)/shard_map/while/body/eval_jaxpr/jk,smko->smjo/dot_general | solution.py:103
  137.3 2.5 fusion.126
  140.5 2.7 %convert_bitcast_fusion.2 = bf16[2,256,16,128]{3,2,1,0:T(8,128)(2,1)S(1)} fusion(bf16[2,256,24,128]{3,2,1,0:T(8,128)(2,1)} %get-tuple-element.467, s32[16]{0:T(128)S(1)} %fusion.125), kind=kOutput, calls=%fused_computation.2.clone.1 | convolution fusion | flops 51380608 | bytes 5242944 | tf_op jit(solution)/shard_map/while/body/eval_jaxpr/jk,smko->smjo/dot_general | solution.py:103
  145.6 2.5 fusion.126
  148.8 2.7 %convert_bitcast_fusion.2 = bf16[2,256,16,128]{3,2,1,0:T(8,128)(2,1)S(1)} fusion(bf16[2,256,24,128]{3,2,1,0:T(8,128)(2,1)} %get-tuple-element.467, s32[16]{0:T(128)S(1)} %fusion.125), kind=kOutput, calls=%fused_computation.2.clone.1 | convolution fusion | flops 51380608 | bytes 5242944 | tf_op jit(solution)/shard_map/while/body/eval_jaxpr/jk,smko->smjo/dot_general | solution.py:103
  153.9 2.5 fusion.126
  157.1 2.7 %convert_bitcast_fusion.2 = bf16[2,256,16,128]{3,2,1,0:T(8,128)(2,1)S(1)} fusion(bf16[2,256,24,128]{3,2,1,0:T(8,128)(2,1)} %get-tuple-element.467, s32[16]{0:T(128)S(1)} %fusion.125), kind=kOutput, calls=%fused_computation.2.clone.1 | convolution fusion | flops 51380608 | bytes 5242944 | tf_op jit(solution)/shard_map/while/body/eval_jaxpr/jk,smko->smjo/dot_general | solution.py:103
  162.2 2.5 fusion.126
  165.4 2.7 %convert_bitcast_fusion.2 = bf16[2,256,16,128]{3,2,1,0:T(8,128)(2,1)S(1)} fusion(bf16[2,256,24,128]{3,2,1,0:T(8,128)(2,1)} %get-tuple-element.467, s32[16]{0:T(128)S(1)} %fusion.125), kind=kOutput, calls=%fused_computation.2.clone.1 | convolution fusion | flops 51380608 | bytes 5242944 | tf_op jit(solution)/shard_map/while/body/eval_jaxpr/jk,smko->smjo/dot_general | solution.py:103
  170.5 2.5 fusion.126
  173.6 2.7 %convert_bitcast_fusion.2 = bf16[2,256,16,128]{3,2,1,0:T(8,128)(2,1)S(1)} fusion(bf16[2,256,24,128]{3,2,1,0:T(8,128)(2,1)} %get-tuple-element.467, s32[16]{0:T(128)S(1)} %fusion.125), kind=kOutput, calls=%fused_computation.2.clone.1 | convolution fusion | flops 51380608 | bytes 5242944 | tf_op jit(solution)/shard_map/while/body/eval_jaxpr/jk,smko->smjo/dot_general | solution.py:103
  178.7 2.5 fusion.126
  181.9 2.7 %convert_bitcast_fusion.2 = bf16[2,256,16,128]{3,2,1,0:T(8,128)(2,1)S(1)} fusion(bf16[2,256,24,128]{3,2,1,0:T(8,128)(2,1)} %get-tuple-element.467, s32[16]{0:T(128)S(1)} %fusion.125), kind=kOutput, calls=%fused_computation.2.clone.1 | convolution fusion | flops 51380608 | bytes 5242944 | tf_op jit(solution)/shard_map/while/body/eval_jaxpr/jk,smko->smjo/dot_general | solution.py:103
  187.0 2.5 fusion.126
  190.2 2.7 %convert_bitcast_fusion.2 = bf16[2,256,16,128]{3,2,1,0:T(8,128)(2,1)S(1)} fusion(bf16[2,256,24,128]{3,2,1,0:T(8,128)(2,1)} %get-tuple-element.467, s32[16]{0:T(128)S(1)} %fusion.125), kind=kOutput, calls=%fused_computation.2.clone.1 | convolution fusion | flops 51380608 | bytes 5242944 | tf_op jit(solution)/shard_map/while/body/eval_jaxpr/jk,smko->smjo/dot_general | solution.py:103
  195.3 2.5 fusion.126
  198.5 2.7 %convert_bitcast_fusion.2 = bf16[2,256,16,128]{3,2,1,0:T(8,128)(2,1)S(1)} fusion(bf16[2,256,24,128]{3,2,1,0:T(8,128)(2,1)} %get-tuple-element.467, s32[16]{0:T(128)S(1)} %fusion.125), kind=kOutput, calls=%fused_computation.2.clone.1 | convolution fusion | flops 51380608 | bytes 5242944 | tf_op jit(solution)/shard_map/while/body/eval_jaxpr/jk,smko->smjo/dot_general | solution.py:103
  203.6 2.5 fusion.126
  206.8 2.7 %convert_bitcast_fusion.2 = bf16[2,256,16,128]{3,2,1,0:T(8,128)(2,1)S(1)} fusion(bf16[2,256,24,128]{3,2,1,0:T(8,128)(2,1)} %get-tuple-element.467, s32[16]{0:T(128)S(1)} %fusion.125), kind=kOutput, calls=%fused_computation.2.clone.1 | convolution fusion | flops 51380608 | bytes 5242944 | tf_op jit(solution)/shard_map/while/body/eval_jaxpr/jk,smko->smjo/dot_general | solution.py:103
  211.9 2.5 fusion.126
  215.1 2.7 %convert_bitcast_fusion.2 = bf16[2,256,16,128]{3,2,1,0:T(8,128)(2,1)S(1)} fusion(bf16[2,256,24,128]{3,2,1,0:T(8,128)(2,1)} %get-tuple-element.467, s32[16]{0:T(128)S(1)} %fusion.125), kind=kOutput, calls=%fused_computation.2.clone.1 | convolution fusion | flops 51380608 | bytes 5242944 | tf_op jit(solution)/shard_map/while/body/eval_jaxpr/jk,smko->smjo/dot_general | solution.py:103
  220.2 2.5 fusion.126
  223.4 2.7 %convert_bitcast_fusion.2 = bf16[2,256,16,128]{3,2,1,0:T(8,128)(2,1)S(1)} fusion(bf16[2,256,24,128]{3,2,1,0:T(8,128)(2,1)} %get-tuple-element.467, s32[16]{0:T(128)S(1)} %fusion.125), kind=kOutput, calls=%fused_computation.2.clone.1 | convolution fusion | flops 51380608 | bytes 5242944 | tf_op jit(solution)/shard_map/while/body/eval_jaxpr/jk,smko->smjo/dot_general | solution.py:103
  228.5 2.5 fusion.126
  231.7 2.7 %convert_bitcast_fusion.2 = bf16[2,256,16,128]{3,2,1,0:T(8,128)(2,1)S(1)} fusion(bf16[2,256,24,128]{3,2,1,0:T(8,128)(2,1)} %get-tuple-element.467, s32[16]{0:T(128)S(1)} %fusion.125), kind=kOutput, calls=%fused_computation.2.clone.1 | convolution fusion | flops 51380608 | bytes 5242944 | tf_op jit(solution)/shard_map/while/body/eval_jaxpr/jk,smko->smjo/dot_general | solution.py:103
  236.8 2.5 fusion.126
  240.8 21.5 %all_to_all.33 = bf16[256,8,256]{2,1,0:T(8,128)(2,1)S(1)} all-to-all(bf16[256,8,256]{2,1,0:T(8,128)(2,1)S(1)} %bitcast.160), channel_id=1, replica_groups=mesh['wide'=32,'lon'=8] {'wide'}, dimensions={0} | all-to-all | bytes 2097152 | tf_op jit(solution)/shard_map/all_to_all | solution.py:118
  (130 shorter events, 56.6 us)
Async XLA Ops:
  0.0 34.9 %copy-start = (f32[4,256,256]{2,1,0:T(8,128)S(1)}, f32[4,256,256]{2,1,0:T(8,128)}, u32[]{:S(2)}) copy-start(f32[4,256,256]{2,1,0:T(8,128)} %param.14) | copy-start | bytes 3145732
  2.2 17.1 %collective-permute-start = (bf16[8,256,1]{2,0,1:T(8,128)(2,1)S(1)}, bf16[8,256,1]{2,0,1:T(8,128)(2,1)S(1)}, u32[]{:S(2)}, u32[]{:S(2)}) collective-permute-start(bf16[8,256,1]{2,0,1:T(8,128)(2,1)S(1)} %get-tuple-element.305), channel_id=1, source_target_pairs={{1,0},{2,1},{3,2},{4,3},{5,4},{6,5},{7,6},{0,7},{9,8},{10,9},{11,1... | collective-permute-start | bytes 12296 | tf_op jit(solution)/shard_map/ppermute | solution.py:20
  8.7 13.7 %collective-permute-start.1 = (bf16[8,256,1]{2,0,1:T(8,128)(2,1)S(1)}, bf16[8,256,1]{2,0,1:T(8,128)(2,1)S(1)}, u32[]{:S(2)}, u32[]{:S(2)}) collective-permute-start(bf16[8,256,1]{2,0,1:T(8,128)(2,1)S(1)} %get-tuple-element.306), channel_id=1, source_target_pairs={{0,1},{1,2},{2,3},{3,4},{4,5},{5,6},{6,7},{7,0},{8,9},{9,10},{10,1... | collective-permute-start | bytes 12296 | tf_op jit(solution)/shard_map/ppermute | solution.py:19
  25.1 26.2 %all-to-all-start = ((bf16[8,256,256]{2,0,1:T(8,128)(2,1)}), bf16[8,256,256]{2,0,1:T(8,128)(2,1)}, u32[]{:S(2)}, u32[]{:S(2)}) async-start(bf16[8,256,256]{2,0,1:T(8,128)(2,1)} %fusion.90), calls=%async_computation | async-start | bytes 2097152 | tf_op jit(solution)/shard_map/all_to_all | solution.py:75
  84.5 14.4 %collective-permute-start.2 = (bf16[2,256,512]{1,2,0:T(8,128)(2,1)S(1)}, bf16[2,256,512]{1,2,0:T(8,128)(2,1)S(1)}, u32[]{:S(2)}, u32[]{:S(2)}) collective-permute-start(bf16[2,256,512]{1,2,0:T(8,128)(2,1)S(1)} %get-tuple-element.301), channel_id=1, source_target_pairs={{0,1},{1,2},{2,3},{3,4},{4,5},{5,6},{6,7},{7,0},{8,9},{9,10},{10,1... | collective-permute-start | bytes 1572872 | tf_op jit(solution)/shard_map/ppermute | solution.py:19
  84.6 14.3 %collective-permute-start.3 = (bf16[2,256,512]{1,2,0:T(8,128)(2,1)S(1)}, bf16[2,256,512]{1,2,0:T(8,128)(2,1)S(1)}, u32[]{:S(2)}, u32[]{:S(2)}) collective-permute-start(bf16[2,256,512]{1,2,0:T(8,128)(2,1)S(1)} %get-tuple-element.302), channel_id=1, source_target_pairs={{1,0},{2,1},{3,2},{4,3},{5,4},{6,5},{7,6},{0,7},{9,8},{10,9},{11,1... | collective-permute-start | bytes 1572872 | tf_op jit(solution)/shard_map/ppermute | solution.py:20
  100.7 5.9 %copy-start.1 = (s32[1,16]{1,0:T(1,128)S(1)}, s32[1,16]{1,0:T(1,128)}, u32[]{:S(2)}) copy-start(s32[1,16]{1,0:T(1,128)} %param.16) | copy-start | bytes 196
where the time goes:
time: 267 us; the launch traced here: 263 us
  matrix products  115 us (43%)
  local copies, waits for them, and re-layouts  38.1 us (14%)
  waiting for transfers between devices  35.9 us (13%)
  other arithmetic  33.8 us (13%)
  blocking collectives  21.5 us (8%)
  starting transfers between devices  18.2 us (7%)
    dot_general x16, matrix products, body_one_block(): jnp.einsum('jk,smko->smjo', selector, cand, preferred_element_type=jnp.fl...  43.1 us
    dot_general x16, matrix products, body_one_block(): jnp.einsum('mjo,jco->mc', picked[1], tapered, preferred_element_type=jnp....  40 us
    dot_general x16, matrix products, observe_one_block(): picked = jnp.dot(state, selector, preferred_element_type=jnp.float32)  31.8 us
    all_to_all x1, blocking collectives, body(): lax.all_to_all(result.reshape(members, band_rows, patch_meridian_lines),...  21.5 us
    all_to_all x1, waiting for transfers between devices, body(): lax.all_to_all(prediction_increment, 'wide', split_axis=1, concat_axis=0,...  14.7 us
    mul x16, other arithmetic, taper_tiles(): length = 8.0 * jnp.exp2(classes.astype(jnp.float32))  11.3 us
    eq x16, local copies, waits for them, and re-layouts, body_one_block(): selector = (candidate_ids == listed[:, None]).astype(jnp.bfloat16)  11.1 us
    ppermute x2, waiting for transfers between devices, padded_2(): before = lax.ppermute(last, axis, up)  10.8 us
  transfers between devices with their start and end apart: 5, of which 4 were waited for; matrix products, arithmetic and copies ran while one was open for 3% of the time, Pallas kernels for 0%

commit v1 on v0

v1 whole, which is shorter than its diff:
```python
import functools

import jax
import jax.numpy as jnp
from jax import lax
from jax.experimental import pallas as pl
from jax.experimental.pallas import tpu as pltpu
from jax.sharding import PartitionSpec as P

MESH = pl.DeviceIdType.MESH
F32 = jnp.float32
BF16 = jnp.bfloat16

M = 256
ROWS = 8
Q = 256
NW = 32
NL = 8
MD = 8
BLK = 128
HALO = 512
CELLS = ROWS * Q
CAND = CELLS + 2 * HALO
PAIR = 2
CHUNKS = ROWS // PAIR


def iota(shape, dim):
    return lax.broadcasted_iota(jnp.int32, shape, dim)


def kernel(
    x_hbm, innov_hbm, idx_hbm, wgt_hbm, list_ref, count_ref, class_ref, out_ref,
    x_in, x_f, edge_out, edge_in, sent, region, innov_in, innov_all, idx, wgt, cols, sel,
    dev, obs_acc, obs_all, table, dense_v, dense_s, tapered, back, home,
    load_sem, edge_send, edge_recv, a_send, a_recv, ih_send, ih_recv, oh_send, oh_recv,
    b_send, b_recv, class_sem,
):
    me = lax.axis_index("wide")
    tile = lax.axis_index("lon")
    east = lax.rem(tile + 1, NL)
    west = lax.rem(tile + NL - 1, NL)

    load_x = pltpu.make_async_copy(x_hbm, x_in, load_sem.at[0])
    load_x.start()
    load_innov = pltpu.make_async_copy(innov_hbm, innov_in, load_sem.at[1])
    load_innov.start()
    first = pl.multiple_of(me * ROWS, ROWS)
    load_idx = pltpu.make_async_copy(idx_hbm.at[:, pl.ds(first, ROWS), :], idx, load_sem.at[2])
    load_idx.start()
    load_wgt = pltpu.make_async_copy(wgt_hbm.at[:, pl.ds(first, ROWS), :], wgt, load_sem.at[3])
    load_wgt.start()

    barrier = pltpu.get_barrier_semaphore()

    def greet(k, carry):
        other = lax.rem(me + k, NW)
        pl.semaphore_signal(barrier, inc=1, device_id={"wide": other}, device_id_type=MESH)
        return carry

    for t in (east, west):
        pl.semaphore_signal(barrier, inc=1, device_id={"lon": t}, device_id_type=MESH)
    lax.fori_loop(1, NW, greet, 0)

    load_x.wait()
    x_f[:, 0:8, :] = jnp.zeros((MD, 8, Q), F32)
    x_f[:, 8 + 256:8 + 256 + 8, :] = jnp.zeros((MD, 8, Q), F32)

    def widen(step, carry):
        r0 = pl.multiple_of(step * 32, 32)
        lane = iota((32, BLK), 1)
        left = jnp.zeros((32, BLK), F32)
        right = jnp.zeros((32, BLK), F32)
        for m in range(MD):
            v = x_in[m, pl.ds(r0, 32), :].astype(F32)
            x_f[m, pl.ds(pl.multiple_of(r0 + 8, 8), 32), :] = v
            a = v[:, :BLK]
            b = v[:, BLK:]
            left = jnp.where(lane == m, pltpu.roll(a, m, 1) if m else a, left)
            right = jnp.where(lane == m, pltpu.roll(b, m + 1, 1), right)
        edge_out[0, pl.ds(r0, 32), :] = left.astype(BF16)
        edge_out[1, pl.ds(r0, 32), :] = right.astype(BF16)
        return carry

    lax.fori_loop(0, 8, widen, 0)

    pl.semaphore_wait(barrier, NW - 1 + 2)

    edges = []
    for side, t in ((0, west), (1, east)):
        copy = pltpu.make_async_remote_copy(
            src_ref=edge_out.at[side], dst_ref=edge_in.at[side],
            send_sem=edge_send.at[side], recv_sem=edge_recv.at[side],
            device_id={"lon": t}, device_id_type=MESH)
        copy.start()
        edges.append(copy)

    d = (iota((BLK, BLK), 0) - iota((BLK, BLK), 1)).astype(F32)
    for c in range(4):
        s = d * (1.0 / (8.0 * 2.0 ** c))
        table[c] = (1.0 / (M - 1.0)) / (1.0 + s * s)
    table[4] = jnp.zeros((BLK, BLK), F32)

    block = iota((16, BLK), 0)
    ids = iota((16, BLK), 1)
    counts = jnp.zeros((16, BLK), jnp.int32)
    for b in range(16):
        counts = jnp.where(block == b, count_ref[0, b], counts)
    listed = list_ref[0]
    classes = class_ref[0]
    dense = jnp.full((16, BLK), 4, jnp.int32)
    for j in range(16):
        hit = (ids == listed[:, j:j + 1]) & (counts > j)
        dense = jnp.where(hit, classes[:, j:j + 1], dense)
    dense_v[...] = dense
    to_scalar = pltpu.make_async_copy(dense_v, dense_s, class_sem)
    to_scalar.start()

    for copy in edges:
        copy.wait()

    def forecast(r, carry):
        r0 = pl.multiple_of(r * ROWS, ROWS)
        lane = iota((ROWS, BLK), 1)
        e_in = edge_in[0, pl.ds(pl.multiple_of(lax.div(r, 2) * 16, 16), 16), :].astype(F32)
        w_in = edge_in[1, pl.ds(pl.multiple_of(lax.div(r, 2) * 16, 16), 16), :].astype(F32)
        odd = lax.rem(r, 2) == 1
        e_in = jnp.where(odd, e_in[8:16], e_in[0:8])
        w_in = jnp.where(odd, w_in[8:16], w_in[0:8])
        halves = [[], []]
        for m in range(MD):
            around = x_f[m, pl.ds(r0, 3 * ROWS), :]
            v, n, s = around[8:16], around[9:17], around[7:15]
            a, b = v[:, :BLK], v[:, BLK:]
            a_up, b_up = pltpu.roll(a, BLK - 1, 1), pltpu.roll(b, BLK - 1, 1)
            a_dn, b_dn = pltpu.roll(a, 1, 1), pltpu.roll(b, 1, 1)
            e_edge = pltpu.roll(e_in, BLK - 1 - m, 1)
            w_edge = pltpu.roll(w_in, (BLK - m) % BLK, 1) if m else w_in
            e_a = jnp.where(lane == BLK - 1, b_up, a_up)
            e_b = jnp.where(lane == BLK - 1, e_edge, b_up)
            w_a = jnp.where(lane == 0, w_edge, a_dn)
            w_b = jnp.where(lane == 0, a_dn, b_dn)
            for h, (c, e, w) in enumerate(((a, e_a, w_a), (b, e_b, w_b))):
                hs = slice(h * BLK, (h + 1) * BLK)
                spread = e + w + n[:, hs] + s[:, hs] - 4.0 * c
                halves[h].append(c + 0.2 * spread - 0.3 * (e - w))
        pieces = [jnp.transpose(jnp.stack(h, axis=0), (1, 0, 2)) for h in halves]
        sent[r] = jnp.concatenate(pieces, axis=1).astype(BF16)
        return carry

    lax.fori_loop(0, NW, forecast, 0)

    own = []
    for j in range(CHUNKS):
        rows = pl.ds(j * PAIR, PAIR)
        copy = pltpu.make_async_copy(sent.at[me, rows], region.at[me, rows], a_recv.at[j])
        copy.start()

        def send(k, carry, rows=rows, j=j):
            other = lax.rem(me + k, NW)
            pltpu.make_async_remote_copy(
                src_ref=sent.at[other, rows], dst_ref=region.at[me, rows],
                send_sem=a_send.at[j], recv_sem=a_recv.at[j],
                device_id={"wide": other}, device_id_type=MESH).start()
            return carry

        lax.fori_loop(1, NW, send, 0)

    load_innov.wait()

    def turn(g, carry):
        m0 = pl.multiple_of(g * 16, 16)
        v = innov_in[pl.ds(m0, 16)].astype(F32)
        parts = [jnp.transpose(v[:8], (1, 0, 2)), jnp.transpose(v[8:], (1, 0, 2))]
        u = jnp.concatenate(parts, axis=1).astype(BF16)
        for r in range(ROWS):
            innov_all[pl.ds(m0, 16), HALO + r * Q:HALO + (r + 1) * Q] = u[r]
        return carry

    lax.fori_loop(0, M // 16, turn, 0)

    def lon_copy(src, dst, send_sem, recv_sem, t):
        copy = pltpu.make_async_remote_copy(
            src_ref=src, dst_ref=dst, send_sem=send_sem, recv_sem=recv_sem,
            device_id={"lon": t}, device_id_type=MESH)
        copy.start()
        return copy

    innov_halo = [
        lon_copy(innov_all.at[:, pl.ds(CELLS, HALO)], innov_all.at[:, pl.ds(0, HALO)],
                 ih_send.at[0], ih_recv.at[0], east),
        lon_copy(innov_all.at[:, pl.ds(HALO, HALO)], innov_all.at[:, pl.ds(HALO + CELLS, HALO)],
                 ih_send.at[1], ih_recv.at[1], west),
    ]

    load_idx.wait()
    load_wgt.wait()
    origin = me * CELLS

    def columns(i, carry):
        parts = [(idx[k, pl.ds(i, 1), :] - origin).astype(F32) for k in range(4)]
        parts += [wgt[k, pl.ds(i, 1), :] for k in range(4)]
        stacked = jnp.concatenate(parts + [jnp.zeros((BLK - 8, Q), F32)], axis=0)
        cols[pl.ds(pl.multiple_of(i * Q, Q), Q), :] = jnp.transpose(stacked, (1, 0))
        return carry

    lax.fori_loop(0, ROWS, columns, 0)

    def select(g, carry):
        o0 = pl.multiple_of(g * 16, 16)
        here = cols[pl.ds(o0, 16), :]
        cell = [jnp.broadcast_to(here[:, k:k + 1], (16, BLK)) for k in range(4)]
        weight = [jnp.broadcast_to(here[:, 4 + k:5 + k], (16, BLK)) for k in range(4)]
        ids = iota((16, BLK), 1).astype(F32)
        for t in range(CELLS // BLK):
            at = ids + float(t * BLK)
            acc = jnp.where(at == cell[0], weight[0], 0.0)
            for k in range(1, 4):
                acc = acc + jnp.where(at == cell[k], weight[k], 0.0)
            sel[pl.ds(o0, 16), t * BLK:(t + 1) * BLK] = acc.astype(BF16)
        return carry

    lax.fori_loop(0, CELLS // 16, select, 0)

    def anomaly(r):
        v = region[:, r].astype(F32)
        for h in range(2):
            u = v[:, h * MD:(h + 1) * MD, :].reshape(M, BLK)
            u = u - jnp.sum(u, axis=0, keepdims=True) * (1.0 / M)
            dev[:, r * Q + h * BLK:r * Q + (h + 1) * BLK] = u.astype(BF16)

    def partial_obs(j, o):
        cells = slice(j * PAIR * Q, (j + 1) * PAIR * Q)
        return lax.dot_general(
            sel[pl.ds(pl.multiple_of(o * Q, Q), Q), cells], dev[:, cells],
            (((1,), (1,)), ((), ())), preferred_element_type=F32)

    for j in range(CHUNKS):
        rows = pl.ds(j * PAIR, PAIR)
        pltpu.make_async_copy(region.at[:, rows], region.at[:, rows], a_recv.at[j]).wait()
        for r in range(j * PAIR, (j + 1) * PAIR):
            anomaly(r)
        if j < CHUNKS - 1:
            def add(o, carry, j=j):
                at = pl.ds(pl.multiple_of(o * Q, Q), Q)
                part = partial_obs(j, o)
                obs_acc[at, :] = part if j == 0 else obs_acc[at, :] + part
                return carry

            lax.fori_loop(0, ROWS, add, 0)

    def finish(o, carry):
        at = pl.ds(pl.multiple_of(o * Q, Q), Q)
        to = pl.ds(pl.multiple_of(o * Q + HALO, Q), Q)
        obs_all[to, :] = (obs_acc[at, :] + partial_obs(CHUNKS - 1, o)).astype(BF16)
        return carry

    lax.fori_loop(0, 2, finish, 0)
    lax.fori_loop(ROWS - 2, ROWS, finish, 0)
    obs_halo = [
        lon_copy(obs_all.at[pl.ds(CELLS, HALO)], obs_all.at[pl.ds(0, HALO)],
                 oh_send.at[0], oh_recv.at[0], east),
        lon_copy(obs_all.at[pl.ds(HALO, HALO)], obs_all.at[pl.ds(HALO + CELLS, HALO)],
                 oh_send.at[1], oh_recv.at[1], west),
    ]
    lax.fori_loop(2, ROWS - 2, finish, 0)

    for copy in innov_halo + obs_halo:
        copy.wait()
    to_scalar.wait()

    def update(r, carry):
        c0 = pl.multiple_of(r * Q, Q)
        right = dev[:, pl.ds(c0, Q)]
        for i in range(CAND // Q):
            cov = jnp.dot(obs_all[i * Q:(i + 1) * Q, :], right, preferred_element_type=F32)
            for oh in range(2):
                for ch in range(2):
                    factor = table[dense_s[2 * r + ch, 2 * i + oh]]
                    part = cov[oh * BLK:(oh + 1) * BLK, ch * BLK:(ch + 1) * BLK] * factor
                    tapered[i * Q + oh * BLK:i * Q + (oh + 1) * BLK, ch * BLK:(ch + 1) * BLK] = part.astype(BF16)
        change = jnp.dot(innov_all[...], tapered[...], preferred_element_type=F32)
        state = region[:, r].astype(F32)
        parts = [
            state[:, h * MD:(h + 1) * MD, :] + change[:, h * BLK:(h + 1) * BLK].reshape(NW, MD, BLK)
            for h in range(2)
        ]
        back[:, r] = jnp.concatenate(parts, axis=1).astype(BF16)
        pltpu.make_async_copy(back.at[me, r], home.at[me, r], b_recv).start()

        def send(k, inner):
            other = lax.rem(me + k, NW)
            pltpu.make_async_remote_copy(
                src_ref=back.at[other, r], dst_ref=home.at[me, r],
                send_sem=b_send, recv_sem=b_recv,
                device_id={"wide": other}, device_id_type=MESH).start()
            return inner

        lax.fori_loop(1, NW, send, 0)
        return carry

    lax.fori_loop(0, ROWS, update, 0)

    pltpu.make_async_copy(home, home, b_recv).wait()

    def settle(g, carry):
        v = home[pl.ds(2 * g, 2)].astype(F32)
        for h in range(2):
            u = v[:, :, h * MD:(h + 1) * MD, :]
            parts = [jnp.transpose(u[0], (1, 0, 2)), jnp.transpose(u[1], (1, 0, 2))]
            out_ref[:, pl.ds(pl.multiple_of(g * 16, 16), 16), h * BLK:(h + 1) * BLK] = (
                jnp.concatenate(parts, axis=1).astype(BF16))
        return carry

    lax.fori_loop(0, NW // 2, settle, 0)

    for j in range(CHUNKS):
        rows = pl.ds(j * PAIR, PAIR)
        some = sent.at[pl.ds(0, NW - 1), rows]
        pltpu.make_async_copy(some, some, a_send.at[j]).wait()
    some = back.at[pl.ds(0, NW - 1)]
    pltpu.make_async_copy(some, some, b_send).wait()


def body(x, innov, obs_index, obs_weight, obs_list, tile_count, taper_class):
    anywhere = pl.BlockSpec(memory_space=pl.ANY)
    vmem = pl.BlockSpec(memory_space=pltpu.VMEM)
    dma = pltpu.SemaphoreType.DMA
    return pl.pallas_call(
        kernel,
        out_shape=jax.ShapeDtypeStruct((MD, 256, Q), BF16),
        in_specs=[anywhere] * 4 + [vmem, pl.BlockSpec(memory_space=pltpu.SMEM), vmem],
        out_specs=vmem,
        scratch_shapes=[
            pltpu.VMEM((MD, 256, Q), BF16),
            pltpu.VMEM((MD, 256 + 16, Q), F32),
            pltpu.VMEM((2, 256, BLK), BF16),
            pltpu.VMEM((2, 256, BLK), BF16),
            pltpu.VMEM((NW, ROWS, 16, BLK), BF16),
            pltpu.VMEM((NW, ROWS, 16, BLK), BF16),
            pltpu.VMEM((M, ROWS, Q), BF16),
            pltpu.VMEM((M, CAND), BF16),
            pltpu.VMEM((4, ROWS, Q), jnp.int32),
            pltpu.VMEM((4, ROWS, Q), F32),
            pltpu.VMEM((CELLS, BLK), F32),
            pltpu.VMEM((CELLS, CELLS), BF16),
            pltpu.VMEM((M, CELLS), BF16),
            pltpu.VMEM((CELLS, M), F32),
            pltpu.VMEM((CAND, M), BF16),
            pltpu.VMEM((5, BLK, BLK), F32),
            pltpu.VMEM((16, BLK), jnp.int32),
            pltpu.SMEM((16, BLK), jnp.int32),
            pltpu.VMEM((CAND, Q), BF16),
            pltpu.VMEM((NW, ROWS, 16, BLK), BF16),
            pltpu.VMEM((NW, ROWS, 16, BLK), BF16),
            dma((4,)), dma((2,)), dma((2,)), dma((CHUNKS,)), dma((CHUNKS,)),
            dma((2,)), dma((2,)), dma((2,)), dma((2,)), dma, dma, dma,
        ],
        compiler_params=pltpu.CompilerParams(
            collective_id=0, has_side_effects=True, vmem_limit_bytes=56 * 1024 * 1024),
    )(x, innov, obs_index, obs_weight, obs_list, tile_count, taper_class)


def solution(mesh):
    in_specs = (
        P("wide", None, "lon"),
        P(None, "wide", "lon"),
        P(None, None, "lon"),
        P(None, None, "lon"),
        P("lon", "wide", None),
        P("lon", "wide"),
        P("lon", "wide", None),
    )
    return jax.shard_map(
        body, mesh=mesh, in_specs=in_specs, out_specs=P("wide", None, "lon"), check_vma=False)
```

time: 267 us -> 78.6 us (0.29); the launches traced: 263 us -> 78.4 us
  matrix products: 115 us -> 0 us
  Pallas kernels: 0 us -> 76.1 us
  waiting for transfers between devices: 35.9 us -> 0 us
  local copies, waits for them, and re-layouts: 38.1 us -> 2.26 us
  other arithmetic: 33.8 us -> 0 us
  blocking collectives: 21.5 us -> 0 us
  starting transfers between devices: 18.2 us -> 0 us
    dot_general x48 -> x0, matrix products: 115 us -> none  [the longest x16 43.1 us: body_one_block(): jnp.einsum('jk,smko->smjo', selector, cand, preferred_element_type=jnp.fl...]
    pallas_call x0 -> x1, Pallas kernels: none -> 76.1 us  [body(): pl.pallas_call(kernel, out_shape=jax.ShapeDtypeStruct((MD, 256, Q), BF16)...]
    all_to_all x1 -> x0, blocking collectives: 21.5 us -> none  [body(): lax.all_to_all(result.reshape(members, band_rows, patch_meridian_lines),...]
    ppermute x4 -> x0, waiting for transfers between devices: 21.2 us -> none  [the longest x2 10.8 us: padded_2(): before = lax.ppermute(last, axis, up)]
    convert_element_type x20 -> x0, other arithmetic: 15.8 us -> none  [the longest x16 10.1 us: body_one_block(): (jnp.arange(listed.shape[0], dtype=jnp.int32) < live_count).astype(jnp.fl...]
    all_to_all x1 -> x0, waiting for transfers between devices: 14.7 us -> none  [body(): lax.all_to_all(prediction_increment, 'wide', split_axis=1, concat_axis=0,...]
    mul x16 -> x0, other arithmetic: 11.3 us -> none  [taper_tiles(): length = 8.0 * jnp.exp2(classes.astype(jnp.float32))]
    eq x16 -> x0, local copies, waits for them, and re-layouts: 11.1 us -> none  [body_one_block(): selector = (candidate_ids == listed[:, None]).astype(jnp.bfloat16)]
  transfers between devices with their start and end apart: 5 -> 0, of which waited for: 4 -> 0; matrix products, arithmetic and copies ran while one was open for 3% -> 0% of each run, Pallas kernels for 0% -> 0%
where the time goes in v1:
time: 78.6 us; the launch traced here: 78.4 us
  Pallas kernels  76.1 us (97%)
  local copies, waits for them, and re-layouts  2.26 us (3%)
    pallas_call x1, Pallas kernels, body(): pl.pallas_call(kernel, out_shape=jax.ShapeDtypeStruct((MD, 256, Q), BF16)...  76.1 us
    unnamed x1, local copies, waits for them, and re-layouts  2.26 us

profile of v1, /device:TPU:1, one launch (start us, length us, event | category | flops | bytes accessed | tf_op | source)
XLA Modules:
  0.0 78.4 jit_solution(287178848036518744)
XLA Ops:
  0.0 76.1 %shard_map.73 = bf16[8,256,256]{2,1,0:T(8,128)(2,1)} custom-call(bf16[8,256,256]{2,1,0:T(8,128)(2,1)} %x_hbm.1, bf16[256,8,256]{2,1,0:T(8,128)(2,1)} %innov_hbm.1, s32[4,256,256]{2,1,0:T(8,128)} %idx_hbm.1, f32[4,256,256]{2,1,0:T(8,128)} %wgt_hbm.1, s32[1,16,16]{2,1,0:T(8,128)} %list_ref.1, s32[1,16]{1,0:T(1,128)} %count_ref.1, s32[1,16,16]{2,1,0:T(8,128)} %class_ref.1), custom_call_target="tpu_custom_call" | custom-call | tf_op jit(solution)/shard_map/pallas_call | solution.py:329
  76.1 2.3 %copy.9 = bf16[8,256,256]{2,1,0:T(8,128)(2,1)} copy(bf16[8,256,256]{2,1,0:T(8,128)(2,1)} %shard_map.73) | data formatting | bytes 2097152

commit v2 on v1

v2 whole, which is shorter than its diff:
```python
import functools

import jax
import jax.numpy as jnp
from jax import lax
from jax.experimental import pallas as pl
from jax.experimental.pallas import tpu as pltpu
from jax.sharding import PartitionSpec as P

MESH = pl.DeviceIdType.MESH
F32 = jnp.float32
BF16 = jnp.bfloat16

M = 256
ROWS = 8
Q = 256
NW = 32
NL = 8
MD = 8
BLK = 128
HALO = 512
CELLS = ROWS * Q
CAND = CELLS + 2 * HALO
CHUNKS = ((0, 4), (4, 4))
OFFSETS = (10, 9, 11, 6, 14, 5, 7, 13, 15, 2, 8, 1, 3, 4, 12)
GROUP = 64


def iota(shape, dim):
    return lax.broadcasted_iota(jnp.int32, shape, dim)


def kernel(
    x_hbm, innov_hbm, idx_hbm, wgt_hbm, list_hbm, count_hbm, class_hbm, home,
    x_in, x_f, edge_out, edge_in, edge_f, sent, region, innov_in, innov_all, idx, wgt, cols, sel,
    dev, obs_acc, obs_all, table, listed, classes, count_s, dense_v, dense_s,
    own0, own1, out0, out1, part, back,
    load_sem, edge_send, edge_recv, a_send, a_recv, ih_send, ih_recv, oh_send, oh_recv,
    b_send, b_recv, class_sem,
):
    me = lax.axis_index("wide")
    tile = lax.axis_index("lon")
    east = lax.rem(tile + 1, NL)
    west = lax.rem(tile + NL - 1, NL)
    core = lax.rem(me, 2)
    my_x = lax.rem(lax.div(me, 2), 4)
    my_y = lax.div(me, 8)

    def chip(k):
        code = jnp.int32(OFFSETS[0])
        for i in range(1, len(OFFSETS)):
            code = jnp.where(k == i, OFFSETS[i], code)
        to_x = lax.rem(my_x + lax.rem(code, 4), 4)
        to_y = lax.rem(my_y + lax.div(code, 4), 4)
        return to_y * 8 + to_x * 2

    first = pl.multiple_of(me * ROWS, ROWS)
    loads = [
        pltpu.make_async_copy(src, dst, load_sem.at[i]) for i, (src, dst) in enumerate((
            (x_hbm, x_in),
            (idx_hbm.at[:, pl.ds(first, ROWS), :], idx),
            (wgt_hbm.at[:, pl.ds(first, ROWS), :], wgt),
            (innov_hbm, innov_in),
            (list_hbm, listed),
            (count_hbm, count_s),
            (class_hbm, classes),
        ))
    ]
    load_x, load_idx, load_wgt, load_innov, load_list, load_count, load_class = loads
    for load in loads:
        load.start()

    barrier = pltpu.get_barrier_semaphore()

    def greet(k, carry):
        other = lax.rem(me + k, NW)
        pl.semaphore_signal(barrier, inc=1, device_id={"wide": other}, device_id_type=MESH)
        return carry

    for t in (east, west):
        pl.semaphore_signal(barrier, inc=1, device_id={"lon": t}, device_id_type=MESH)
    lax.fori_loop(1, NW, greet, 0)

    x_f[:, 0:8, :] = jnp.zeros((MD, 8, Q), F32)
    x_f[:, 8 + 256:8 + 256 + 8, :] = jnp.zeros((MD, 8, Q), F32)
    load_x.wait()

    def widen(g, carry):
        left, right = carry
        r0 = pl.multiple_of(g * 32, 32)
        lane = iota((32, BLK), 1) - g * 8
        a_new = jnp.zeros((32, BLK), F32)
        b_new = jnp.zeros((32, BLK), F32)
        lane0 = iota((32, BLK), 1)
        for m in range(MD):
            v = x_in[m, pl.ds(r0, 32), :].astype(F32)
            x_f[m, pl.ds(pl.multiple_of(r0 + 8, 8), 32), :] = v
            a = v[:, :BLK]
            b = v[:, BLK:]
            a_new = jnp.where(lane0 == m, pltpu.roll(a, m, 1) if m else a, a_new)
            b_new = jnp.where(lane0 == m, pltpu.roll(b, m + 1, 1), b_new)
        here = (lane >= 0) & (lane < MD)
        left = jnp.where(here, pltpu.roll(a_new, g * 8, 1), left)
        right = jnp.where(here, pltpu.roll(b_new, g * 8, 1), right)
        return left, right

    zeros = jnp.zeros((32, BLK), F32)
    left, right = lax.fori_loop(0, 8, widen, (zeros, zeros))
    edge_out[0] = left.astype(BF16)
    edge_out[1] = right.astype(BF16)

    d = (iota((BLK, BLK), 0) - iota((BLK, BLK), 1)).astype(F32)
    for c in range(4):
        s = d * (1.0 / (8.0 * 2.0 ** c))
        table[c] = (1.0 / (M - 1.0)) / (1.0 + s * s)
    table[4] = jnp.zeros((BLK, BLK), F32)

    load_idx.wait()
    load_wgt.wait()
    origin = me * CELLS

    def columns(i, carry):
        parts = [(idx[k, pl.ds(i, 1), :] - origin).astype(F32) for k in range(4)]
        parts += [wgt[k, pl.ds(i, 1), :] for k in range(4)]
        stacked = jnp.concatenate(parts + [jnp.zeros((BLK - 8, Q), F32)], axis=0)
        cols[pl.ds(pl.multiple_of(i * Q, Q), Q), :] = jnp.transpose(stacked, (1, 0))
        return carry

    lax.fori_loop(0, ROWS, columns, 0, unroll=2)

    pl.semaphore_wait(barrier, NW - 1 + 2)

    def lon_copy(src, dst, send_sem, recv_sem, t):
        copy = pltpu.make_async_remote_copy(
            src_ref=src, dst_ref=dst, send_sem=send_sem, recv_sem=recv_sem,
            device_id={"lon": t}, device_id_type=MESH)
        copy.start()
        return copy

    edges = [
        lon_copy(edge_out.at[side], edge_in.at[side], edge_send.at[side], edge_recv.at[side], t)
        for side, t in ((0, west), (1, east))
    ]

    load_innov.wait()

    def turn(g, carry):
        m0 = pl.multiple_of(g * 16, 16)
        v = innov_in[pl.ds(m0, 16)].astype(F32)
        parts = [jnp.transpose(v[:8], (1, 0, 2)), jnp.transpose(v[8:], (1, 0, 2))]
        u = jnp.concatenate(parts, axis=1).astype(BF16)
        for r in range(ROWS):
            innov_all[pl.ds(m0, 16), HALO + r * Q:HALO + (r + 1) * Q] = u[r]
        return carry

    lax.fori_loop(0, M // 16, turn, 0)
    innov_halo = [
        lon_copy(innov_all.at[:, pl.ds(CELLS, HALO)], innov_all.at[:, pl.ds(0, HALO)],
                 ih_send.at[0], ih_recv.at[0], east),
        lon_copy(innov_all.at[:, pl.ds(HALO, HALO)], innov_all.at[:, pl.ds(HALO + CELLS, HALO)],
                 ih_send.at[1], ih_recv.at[1], west),
    ]

    for load in (load_list, load_count, load_class):
        load.wait()
    block = iota((16, BLK), 0)
    ids = iota((16, BLK), 1)
    counts = jnp.zeros((16, BLK), jnp.int32)
    for b in range(16):
        counts = jnp.where(block == b, count_s[0, b], counts)
    dense = jnp.full((16, BLK), 4, jnp.int32)
    for j in range(16):
        hit = (ids == listed[0, :, j:j + 1]) & (counts > j)
        dense = jnp.where(hit, classes[0, :, j:j + 1], dense)
    dense_v[...] = dense
    to_scalar = pltpu.make_async_copy(dense_v, dense_s, class_sem)
    to_scalar.start()

    def select(g, carry):
        o0 = pl.multiple_of(g * GROUP, GROUP)
        here = cols[pl.ds(o0, GROUP), :]
        cell = [jnp.broadcast_to(here[:, k:k + 1], (GROUP, BLK)).astype(jnp.int32) for k in range(4)]
        row = [lax.shift_right_logical(c, 8).astype(F32).astype(BF16) for c in cell]
        col = [(c & (Q - 1)).astype(F32).astype(BF16) for c in cell]
        weight = [jnp.broadcast_to(here[:, 4 + k:5 + k], (GROUP, BLK)).astype(BF16) for k in range(4)]
        lanes = iota((GROUP, BLK), 1).astype(F32)
        none = jnp.zeros((GROUP, BLK), BF16)
        for r in range(ROWS):
            w = [jnp.where(row[k] == jnp.bfloat16(r), weight[k], none) for k in range(4)]
            for h in range(2):
                at = (lanes + float(h * BLK)).astype(BF16)
                acc = jnp.where(at == col[0], w[0], none)
                for k in range(1, 4):
                    acc = acc + jnp.where(at == col[k], w[k], none)
                sel[pl.ds(o0, GROUP), r * Q + h * BLK:r * Q + (h + 1) * BLK] = acc
        return carry

    steps = CELLS // GROUP
    lax.fori_loop(0, steps // 4, select, 0)

    for copy in edges:
        copy.wait()
    edge_f[...] = edge_in[...].astype(F32)

    def forecast(r):
        r0 = pl.multiple_of(r * ROWS, ROWS)
        lane = iota((ROWS, BLK), 1)
        sub = pl.ds(pl.multiple_of(lax.rem(r, 4) * ROWS, ROWS), ROWS)
        turns = lax.rem(BLK - lax.div(r, 4) * 8, BLK)
        e_in = pltpu.roll(edge_f[0, sub, :], turns, 1)
        w_in = pltpu.roll(edge_f[1, sub, :], turns, 1)
        halves = [[], []]
        for m in range(MD):
            around = x_f[m, pl.ds(r0, 3 * ROWS), :]
            v, n, s = around[8:16], around[9:17], around[7:15]
            a, b = v[:, :BLK], v[:, BLK:]
            a_up, b_up = pltpu.roll(a, BLK - 1, 1), pltpu.roll(b, BLK - 1, 1)
            a_dn, b_dn = pltpu.roll(a, 1, 1), pltpu.roll(b, 1, 1)
            e_edge = pltpu.roll(e_in, BLK - 1 - m, 1)
            w_edge = pltpu.roll(w_in, BLK - m, 1) if m else w_in
            e_a = jnp.where(lane == BLK - 1, b_up, a_up)
            e_b = jnp.where(lane == BLK - 1, e_edge, b_up)
            w_a = jnp.where(lane == 0, w_edge, a_dn)
            w_b = jnp.where(lane == 0, a_dn, b_dn)
            for h, (c, e, w) in enumerate(((a, e_a, w_a), (b, e_b, w_b))):
                hs = slice(h * BLK, (h + 1) * BLK)
                spread = e + w + n[:, hs] + s[:, hs] - 4.0 * c
                halves[h].append(c + 0.2 * spread - 0.3 * (e - w))
        pieces = [jnp.transpose(jnp.stack(h, axis=0), (1, 0, 2)) for h in halves]
        sent[r] = jnp.concatenate(pieces, axis=1).astype(BF16)

    def send_forecast(other, j):
        rows = pl.ds(*CHUNKS[j])
        pltpu.make_async_remote_copy(
            src_ref=sent.at[other, rows], dst_ref=region.at[me, rows],
            send_sem=a_send.at[j], recv_sem=a_recv.at[j],
            device_id={"wide": other}, device_id_type=MESH).start()

    def send_near(other, c, j):
        rows = pl.ds(*CHUNKS[j])

        @pl.when(core == c)
        def _():
            pltpu.make_async_copy(sent.at[me, rows], region.at[me, rows], a_recv.at[j]).start()

        @pl.when(core != c)
        def _():
            send_forecast(other, j)

    for c in range(2):
        def compute_send(k, carry, c=c):
            other = chip(k) + c
            forecast(other)
            send_forecast(other, 0)
            return carry

        lax.fori_loop(0, len(OFFSETS), compute_send, 0)
        near = lax.div(me, 2) * 2 + c
        forecast(near)
        sibling = lax.div(me, 2) * 2 + 1 - core
        send_near(sibling, c, 0)
        for j in range(1, len(CHUNKS)):
            def send_rest(k, carry, c=c, j=j):
                send_forecast(chip(k) + c, j)
                return carry

            lax.fori_loop(0, len(OFFSETS), send_rest, 0)
            send_near(sibling, c, j)

    lax.fori_loop(steps // 4, steps, select, 0, unroll=2)

    def anomaly(r):
        v = region[:, r].astype(F32)
        for h in range(2):
            u = v[:, h * MD:(h + 1) * MD, :].reshape(M, BLK)
            u = u - jnp.sum(u, axis=0, keepdims=True) * (1.0 / M)
            dev[:, r * Q + h * BLK:r * Q + (h + 1) * BLK] = u.astype(BF16)

    for j, (row0, rows) in enumerate(CHUNKS):
        arrived = region.at[:, pl.ds(row0, rows)]
        pltpu.make_async_copy(arrived, arrived, a_recv.at[j]).wait()
        for r in range(row0, row0 + rows):
            anomaly(r)
        cells = slice(row0 * Q, (row0 + rows) * Q)

        def product(o0, n, cells=cells):
            return lax.dot_general(
                sel[o0:o0 + n, cells], dev[:, cells],
                (((1,), (1,)), ((), ())), preferred_element_type=F32)

        if j == 0:
            obs_acc[...] = product(0, CELLS)
        elif j < len(CHUNKS) - 1:
            obs_acc[...] += product(0, CELLS)
        else:
            for o0 in (0, CELLS - HALO):
                total = obs_acc[o0:o0 + HALO, :] + product(o0, HALO)
                obs_all[HALO + o0:HALO + o0 + HALO, :] = total.astype(BF16)
            obs_halo = [
                lon_copy(obs_all.at[pl.ds(CELLS, HALO)], obs_all.at[pl.ds(0, HALO)],
                         oh_send.at[0], oh_recv.at[0], east),
                lon_copy(obs_all.at[pl.ds(HALO, HALO)], obs_all.at[pl.ds(HALO + CELLS, HALO)],
                         oh_send.at[1], oh_recv.at[1], west),
            ]
            total = obs_acc[HALO:CELLS - HALO, :] + product(HALO, CELLS - 2 * HALO)
            obs_all[2 * HALO:CELLS, :] = total.astype(BF16)

    to_scalar.wait()

    def covariance(r, candidates, tapered):
        right = dev[:, pl.ds(pl.multiple_of(r * Q, Q), Q)]
        for n, i in enumerate(candidates):
            cov = jnp.dot(obs_all[i * Q:(i + 1) * Q, :], right, preferred_element_type=F32)
            for oh in range(2):
                for ch in range(2):
                    factor = table[dense_s[2 * r + ch, 2 * i + oh]]
                    some = cov[oh * BLK:(oh + 1) * BLK, ch * BLK:(ch + 1) * BLK] * factor
                    tapered[n * Q + oh * BLK:n * Q + (oh + 1) * BLK, ch * BLK:(ch + 1) * BLK] = some.astype(BF16)

    def pipelined(cov, change, after):
        cov(0, 0)

        def step(p, carry):
            change(2 * p, 0)
            cov(2 * p + 1, 1)
            change(2 * p + 1, 1)
            cov(2 * p + 2, 0)
            after(p)
            return carry

        lax.fori_loop(0, ROWS // 2 - 1, step, 0)
        change(ROWS - 2, 0)
        cov(ROWS - 1, 1)
        change(ROWS - 1, 1)
        after(ROWS // 2 - 1)

    own = (own0, own1)

    def own_change(r, slot):
        part[r] = jnp.dot(innov_all[:, HALO:HALO + CELLS], own[slot][...], preferred_element_type=F32)

    pipelined(lambda r, slot: covariance(r, range(2, 10), own[slot]), own_change, lambda p: None)

    for copy in innov_halo + obs_halo:
        copy.wait()
    outer = (out0, out1)

    def outer_change(r, slot):
        change = part[r] + jnp.dot(innov_all[:, 0:HALO], outer[slot][0:HALO, :], preferred_element_type=F32)
        change += jnp.dot(innov_all[:, HALO + CELLS:], outer[slot][HALO:, :], preferred_element_type=F32)
        state = region[:, r].astype(F32)
        parts = [
            state[:, h * MD:(h + 1) * MD, :] + change[:, h * BLK:(h + 1) * BLK].reshape(NW, MD, BLK)
            for h in range(2)
        ]
        back[:, r] = jnp.concatenate(parts, axis=1).astype(BF16)

    def send_pair(p):
        rows = pl.ds(2 * p, 2)

        def send_back(other):
            pltpu.make_async_remote_copy(
                src_ref=back.at[other, rows], dst_ref=home.at[me, rows],
                send_sem=b_send, recv_sem=b_recv,
                device_id={"wide": other}, device_id_type=MESH).start()

        def send(k, carry):
            other = chip(k)
            send_back(other)
            send_back(other + 1)
            return carry

        lax.fori_loop(0, len(OFFSETS), send, 0)
        send_back(sibling)
        pltpu.make_async_copy(back.at[me, rows], home.at[me, rows], b_recv).start()

    pipelined(lambda r, slot: covariance(r, (0, 1, 10, 11), outer[slot]), outer_change, send_pair)

    for j, (row0, rows) in enumerate(CHUNKS):
        some = sent.at[pl.ds(0, NW - 1), pl.ds(row0, rows)]
        pltpu.make_async_copy(some, some, a_send.at[j]).wait()
    some = back.at[pl.ds(0, NW - 1)]
    pltpu.make_async_copy(some, some, b_send).wait()
    pltpu.make_async_copy(home, home, b_recv).wait()


def settle(home_ref, out_ref):
    def pair(g, carry):
        v = home_ref[pl.ds(2 * g, 2)].astype(F32)
        for h in range(2):
            u = v[:, :, h * MD:(h + 1) * MD, :]
            parts = [jnp.transpose(u[0], (1, 0, 2)), jnp.transpose(u[1], (1, 0, 2))]
            out_ref[:, pl.ds(pl.multiple_of(g * 16, 16), 16), h * BLK:(h + 1) * BLK] = (
                jnp.concatenate(parts, axis=1).astype(BF16))
        return carry

    lax.fori_loop(0, home_ref.shape[0] // 2, pair, 0, unroll=2)


def body(x, innov, obs_index, obs_weight, obs_list, tile_count, taper_class):
    anywhere = pl.BlockSpec(memory_space=pl.ANY)
    dma = pltpu.SemaphoreType.DMA
    home = pl.pallas_call(
        kernel,
        out_shape=jax.ShapeDtypeStruct((NW, ROWS, 16, BLK), BF16),
        in_specs=[pl.BlockSpec(memory_space=pltpu.HBM)] * 7,
        out_specs=anywhere,
        scratch_shapes=[
            pltpu.VMEM((MD, 256, Q), BF16),
            pltpu.VMEM((MD, 256 + 16, Q), F32),
            pltpu.VMEM((2, 32, BLK), BF16),
            pltpu.VMEM((2, 32, BLK), BF16),
            pltpu.VMEM((2, 32, BLK), F32),
            pltpu.VMEM((NW, ROWS, 16, BLK), BF16),
            pltpu.VMEM((NW, ROWS, 16, BLK), BF16),
            pltpu.VMEM((M, ROWS, Q), BF16),
            pltpu.VMEM((M, CAND), BF16),
            pltpu.VMEM((4, ROWS, Q), jnp.int32),
            pltpu.VMEM((4, ROWS, Q), F32),
            pltpu.VMEM((CELLS, BLK), F32),
            pltpu.VMEM((CELLS, CELLS), BF16),
            pltpu.VMEM((M, CELLS), BF16),
            pltpu.VMEM((CELLS, M), F32),
            pltpu.VMEM((CAND, M), BF16),
            pltpu.VMEM((5, BLK, BLK), F32),
            pltpu.VMEM((1, 16, 16), jnp.int32),
            pltpu.VMEM((1, 16, 16), jnp.int32),
            pltpu.SMEM((1, 16), jnp.int32),
            pltpu.VMEM((16, BLK), jnp.int32),
            pltpu.SMEM((16, BLK), jnp.int32),
            pltpu.VMEM((CELLS, Q), BF16),
            pltpu.VMEM((CELLS, Q), BF16),
            pltpu.VMEM((2 * HALO, Q), BF16),
            pltpu.VMEM((2 * HALO, Q), BF16),
            pltpu.VMEM((ROWS, M, Q), F32),
            pltpu.VMEM((NW, ROWS, 16, BLK), BF16),
            dma((7,)), dma((2,)), dma((2,)), dma((len(CHUNKS),)), dma((len(CHUNKS),)),
            dma((2,)), dma((2,)), dma((2,)), dma((2,)), dma, dma, dma,
        ],
        compiler_params=pltpu.CompilerParams(
            collective_id=0, has_side_effects=True, vmem_limit_bytes=62 * 1024 * 1024),
    )(x, innov, obs_index, obs_weight, obs_list, tile_count, taper_class)
    part = 8
    return pl.pallas_call(
        settle,
        out_shape=jax.ShapeDtypeStruct((MD, 256, Q), BF16),
        grid=(NW // part,),
        in_specs=[pl.BlockSpec((part, ROWS, 16, BLK), lambda i: (i, 0, 0, 0))],
        out_specs=pl.BlockSpec((MD, part * ROWS, Q), lambda i: (0, i, 0)),
    )(home)


def solution(mesh):
    in_specs = (
        P("wide", None, "lon"),
        P(None, "wide", "lon"),
        P(None, None, "lon"),
        P(None, None, "lon"),
        P("lon", "wide", None),
        P("lon", "wide"),
        P("lon", "wide", None),
    )
    return jax.shard_map(
        body, mesh=mesh, in_specs=in_specs, out_specs=P("wide", None, "lon"), check_vma=False)
```

time: 78.6 us -> 56.9 us (0.72)
  Pallas kernels: 76.1 us -> 56.7 us
  local copies, waits for them, and re-layouts: 2.26 us -> 0 us
    pallas_call x1 -> x2, Pallas kernels: 76.1 us -> 56.7 us  [the longest x1 53.1 us: body(): pl.pallas_call(kernel, out_shape=jax.ShapeDtypeStruct((NW, ROWS, 16, BLK)...]
    unnamed x1 -> x0, local copies, waits for them, and re-layouts: 2.26 us -> none
where the time goes in v2:
time: 56.9 us; the launch traced here: 56.7 us
  Pallas kernels  56.7 us (100%)
    pallas_call x1, Pallas kernels, body(): pl.pallas_call(kernel, out_shape=jax.ShapeDtypeStruct((NW, ROWS, 16, BLK)...  53.1 us
    pallas_call x1, Pallas kernels, body(): pl.pallas_call(settle, out_shape=jax.ShapeDtypeStruct((MD, 256, Q), BF16)...  3.59 us

profile of v2, /device:TPU:1, one launch (start us, length us, event | category | flops | bytes accessed | tf_op | source)
XLA Modules:
  0.0 56.7 jit_solution(15685984434693361165)
XLA Ops:
  0.0 53.1 %shard_map.73.home_ref = bf16[32,8,16,128]{3,2,1,0:T(8,128)(2,1)} custom-call(bf16[8,256,256]{2,1,0:T(8,128)(2,1)} %x_hbm.1, bf16[256,8,256]{2,1,0:T(8,128)(2,1)} %innov_hbm.1, s32[4,256,256]{2,1,0:T(8,128)} %idx_hbm.1, f32[4,256,256]{2,1,0:T(8,128)} %wgt_hbm.1, s32[1,16,16]{2,1,0:T(8,128)} %list_hbm.1, s32[1,16]{1,0:T(1,128)} %count_hbm.1, ...), custom_call_target="tpu_custom_call" | custom-call | tf_op jit(solution)/shard_map/pallas_call | solution.py:403
  53.1 3.6 %shard_map.74 = bf16[8,256,256]{2,1,0:T(8,128)(2,1)} custom-call(bf16[32,8,16,128]{3,2,1,0:T(8,128)(2,1)} %shard_map.73.home_ref), custom_call_target="tpu_custom_call" | custom-call | tf_op jit(solution)/shard_map/pallas_call | solution.py:444

commit v3 on v2

--- a/solution.py
+++ b/solution.py
@@ -21,8 +21,10 @@
 HALO = 512
 CELLS = ROWS * Q
 CAND = CELLS + 2 * HALO
-CHUNKS = ((0, 4), (4, 4))
-OFFSETS = (10, 9, 11, 6, 14, 5, 7, 13, 15, 2, 8, 1, 3, 4, 12)
+CHUNKS = 2
+PAIR = ROWS // CHUNKS
+CHIPS = 16
+EARLY = 12
 GROUP = 64
 
 
@@ -47,11 +49,11 @@
     my_y = lax.div(me, 8)
 
     def chip(k):
-        code = jnp.int32(OFFSETS[0])
-        for i in range(1, len(OFFSETS)):
-            code = jnp.where(k == i, OFFSETS[i], code)
-        to_x = lax.rem(my_x + lax.rem(code, 4), 4)
-        to_y = lax.rem(my_y + lax.div(code, 4), 4)
+        def offset(i):
+            return jnp.where(i == 0, 2, jnp.where(i == 3, 0, 2 * i - 1))
+
+        to_y = lax.rem(my_y + offset(lax.div(k, 4)), 4)
+        to_x = lax.rem(my_x + offset(lax.rem(k, 4)), 4)
         return to_y * 8 + to_x * 2
 
     first = pl.multiple_of(me * ROWS, ROWS)
@@ -81,33 +83,38 @@
         pl.semaphore_signal(barrier, inc=1, device_id={"lon": t}, device_id_type=MESH)
     lax.fori_loop(1, NW, greet, 0)
 
-    x_f[:, 0:8, :] = jnp.zeros((MD, 8, Q), F32)
-    x_f[:, 8 + 256:8 + 256 + 8, :] = jnp.zeros((MD, 8, Q), F32)
+    x_f[0] = jnp.zeros((MD, Q), F32)
+    x_f[257] = jnp.zeros((MD, Q), F32)
     load_x.wait()
 
     def widen(g, carry):
-        left, right = carry
-        r0 = pl.multiple_of(g * 32, 32)
-        lane = iota((32, BLK), 1) - g * 8
-        a_new = jnp.zeros((32, BLK), F32)
-        b_new = jnp.zeros((32, BLK), F32)
-        lane0 = iota((32, BLK), 1)
-        for m in range(MD):
-            v = x_in[m, pl.ds(r0, 32), :].astype(F32)
-            x_f[m, pl.ds(pl.multiple_of(r0 + 8, 8), 32), :] = v
-            a = v[:, :BLK]
-            b = v[:, BLK:]
-            a_new = jnp.where(lane0 == m, pltpu.roll(a, m, 1) if m else a, a_new)
-            b_new = jnp.where(lane0 == m, pltpu.roll(b, m + 1, 1), b_new)
-        here = (lane >= 0) & (lane < MD)
-        left = jnp.where(here, pltpu.roll(a_new, g * 8, 1), left)
-        right = jnp.where(here, pltpu.roll(b_new, g * 8, 1), right)
-        return left, right
-
-    zeros = jnp.zeros((32, BLK), F32)
-    left, right = lax.fori_loop(0, 8, widen, (zeros, zeros))
-    edge_out[0] = left.astype(BF16)
-    edge_out[1] = right.astype(BF16)
+        r0 = pl.multiple_of(g * 16, 16)
+        v = x_in[:, pl.ds(r0, 16), :].astype(F32)
+        lane = iota((MD, BLK), 1)
+        firsts = jnp.zeros((MD, BLK), F32)
+        lasts = jnp.zeros((MD, BLK), F32)
+        for i in range(0, 16, 8):
+            a = jnp.transpose(v[:, i:i + 8, :BLK], (1, 0, 2))
+            b = jnp.transpose(v[:, i:i + 8, BLK:], (1, 0, 2))
+            x_f[pl.ds(r0 + i + 1, 8)] = jnp.concatenate([a, b], axis=2)
+            for j in range(8):
+                k = i + j
+                firsts = jnp.where(lane == k, pltpu.roll(a[j], k, 1) if k else a[j], firsts)
+                lasts = jnp.where(lane == k, pltpu.roll(b[j], k + 1, 1), lasts)
+        turns = lax.rem(g, 8) * 16
+        wide_lane = iota((MD, Q), 1) - r0
+        here = (wide_lane >= 0) & (wide_lane < 16)
+
+        def place(new, old):
+            new = pltpu.roll(new, turns, 1)
+            return jnp.where(here, jnp.concatenate([new, new], axis=1), old)
+
+        return place(firsts, carry[0]), place(lasts, carry[1])
+
+    zeros = jnp.zeros((MD, Q), F32)
+    left, right = lax.fori_loop(0, 16, widen, (zeros, zeros), unroll=2)
+    edge_out[0] = jnp.concatenate([left, zeros], axis=0).astype(BF16)
+    edge_out[1] = jnp.concatenate([right, zeros], axis=0).astype(BF16)
 
     d = (iota((BLK, BLK), 0) - iota((BLK, BLK), 1)).astype(F32)
     for c in range(4):
@@ -179,136 +186,148 @@
     def select(g, carry):
         o0 = pl.multiple_of(g * GROUP, GROUP)
         here = cols[pl.ds(o0, GROUP), :]
-        cell = [jnp.broadcast_to(here[:, k:k + 1], (GROUP, BLK)).astype(jnp.int32) for k in range(4)]
-        row = [lax.shift_right_logical(c, 8).astype(F32).astype(BF16) for c in cell]
-        col = [(c & (Q - 1)).astype(F32).astype(BF16) for c in cell]
+        cell = [jnp.broadcast_to(here[:, k:k + 1], (GROUP, BLK)) for k in range(4)]
+        cell = [c.astype(jnp.int32).astype(jnp.int16) for c in cell]
         weight = [jnp.broadcast_to(here[:, 4 + k:5 + k], (GROUP, BLK)).astype(BF16) for k in range(4)]
-        lanes = iota((GROUP, BLK), 1).astype(F32)
         none = jnp.zeros((GROUP, BLK), BF16)
-        for r in range(ROWS):
-            w = [jnp.where(row[k] == jnp.bfloat16(r), weight[k], none) for k in range(4)]
-            for h in range(2):
-                at = (lanes + float(h * BLK)).astype(BF16)
-                acc = jnp.where(at == col[0], w[0], none)
-                for k in range(1, 4):
-                    acc = acc + jnp.where(at == col[k], w[k], none)
-                sel[pl.ds(o0, GROUP), r * Q + h * BLK:r * Q + (h + 1) * BLK] = acc
+        sums = []
+        for k in range(4):
+            total = weight[k]
+            for j in range(k):
+                total = total + jnp.where(cell[j] == cell[k], weight[j], none)
+            sums.append(total)
+        lanes = iota((GROUP, BLK), 1).astype(jnp.int16)
+        for t in range(CELLS // BLK):
+            at = lanes + jnp.int16(t * BLK)
+            value = jnp.where(at == cell[0], sums[0], none)
+            for k in range(1, 4):
+                value = jnp.where(at == cell[k], sums[k], value)
+            sel[pl.ds(o0, GROUP), t * BLK:(t + 1) * BLK] = value
         return carry
 
     steps = CELLS // GROUP
-    lax.fori_loop(0, steps // 4, select, 0)
+    lax.fori_loop(0, EARLY, select, 0, unroll=2)
 
     for copy in edges:
         copy.wait()
-    edge_f[...] = edge_in[...].astype(F32)
+    for side in range(2):
+        got = edge_in[side].astype(F32)
+        for h in range(2):
+            edge_f[side, h] = got[:MD, h * BLK:(h + 1) * BLK]
 
     def forecast(r):
-        r0 = pl.multiple_of(r * ROWS, ROWS)
-        lane = iota((ROWS, BLK), 1)
-        sub = pl.ds(pl.multiple_of(lax.rem(r, 4) * ROWS, ROWS), ROWS)
-        turns = lax.rem(BLK - lax.div(r, 4) * 8, BLK)
-        e_in = pltpu.roll(edge_f[0, sub, :], turns, 1)
-        w_in = pltpu.roll(edge_f[1, sub, :], turns, 1)
-        halves = [[], []]
-        for m in range(MD):
-            around = x_f[m, pl.ds(r0, 3 * ROWS), :]
-            v, n, s = around[8:16], around[9:17], around[7:15]
+        lane = iota((MD, BLK), 1)
+        turns = lax.rem(BLK - lax.rem(r, 16) * 8, BLK)
+        e_in = pltpu.roll(edge_f[0, lax.div(r, 16)], turns, 1)
+        w_in = pltpu.roll(edge_f[1, lax.div(r, 16)], turns, 1)
+        for i in range(ROWS):
+            at = r * ROWS + i
+            s, v, n = x_f[at], x_f[at + 1], x_f[at + 2]
             a, b = v[:, :BLK], v[:, BLK:]
             a_up, b_up = pltpu.roll(a, BLK - 1, 1), pltpu.roll(b, BLK - 1, 1)
             a_dn, b_dn = pltpu.roll(a, 1, 1), pltpu.roll(b, 1, 1)
-            e_edge = pltpu.roll(e_in, BLK - 1 - m, 1)
-            w_edge = pltpu.roll(w_in, BLK - m, 1) if m else w_in
+            e_edge = pltpu.roll(e_in, BLK - 1 - i, 1)
+            w_edge = pltpu.roll(w_in, BLK - i, 1) if i else w_in
             e_a = jnp.where(lane == BLK - 1, b_up, a_up)
             e_b = jnp.where(lane == BLK - 1, e_edge, b_up)
             w_a = jnp.where(lane == 0, w_edge, a_dn)
             w_b = jnp.where(lane == 0, a_dn, b_dn)
+            halves = []
             for h, (c, e, w) in enumerate(((a, e_a, w_a), (b, e_b, w_b))):
                 hs = slice(h * BLK, (h + 1) * BLK)
                 spread = e + w + n[:, hs] + s[:, hs] - 4.0 * c
-                halves[h].append(c + 0.2 * spread - 0.3 * (e - w))
-        pieces = [jnp.transpose(jnp.stack(h, axis=0), (1, 0, 2)) for h in halves]
-        sent[r] = jnp.concatenate(pieces, axis=1).astype(BF16)
+                halves.append(c + 0.2 * spread - 0.3 * (e - w))
+            sent[r, i] = jnp.concatenate(halves, axis=0).astype(BF16)
 
     def send_forecast(other, j):
-        rows = pl.ds(*CHUNKS[j])
-        pltpu.make_async_remote_copy(
-            src_ref=sent.at[other, rows], dst_ref=region.at[me, rows],
-            send_sem=a_send.at[j], recv_sem=a_recv.at[j],
-            device_id={"wide": other}, device_id_type=MESH).start()
-
-    def send_near(other, c, j):
-        rows = pl.ds(*CHUNKS[j])
-
-        @pl.when(core == c)
+        rows = pl.ds(j * PAIR, PAIR)
+
+        @pl.when(other == me)
         def _():
             pltpu.make_async_copy(sent.at[me, rows], region.at[me, rows], a_recv.at[j]).start()
 
-        @pl.when(core != c)
+        @pl.when(other != me)
         def _():
-            send_forecast(other, j)
-
-    for c in range(2):
-        def compute_send(k, carry, c=c):
-            other = chip(k) + c
-            forecast(other)
-            send_forecast(other, 0)
-            return carry
-
-        lax.fori_loop(0, len(OFFSETS), compute_send, 0)
-        near = lax.div(me, 2) * 2 + c
-        forecast(near)
-        sibling = lax.div(me, 2) * 2 + 1 - core
-        send_near(sibling, c, 0)
-        for j in range(1, len(CHUNKS)):
-            def send_rest(k, carry, c=c, j=j):
+            pltpu.make_async_remote_copy(
+                src_ref=sent.at[other, rows], dst_ref=region.at[me, rows],
+                send_sem=a_send.at[j], recv_sem=a_recv.at[j],
+                device_id={"wide": other}, device_id_type=MESH).start()
+
+    def phase(c, carry):
+        def compute_send(p, inner):
+            others = [chip(2 * p) + c, chip(2 * p + 1) + c]
+            for other in others:
+                forecast(other)
+            for other in others:
+                send_forecast(other, 0)
+            return inner
+
+        lax.fori_loop(0, CHIPS // 2, compute_send, 0)
+
+        def send_rest(k, inner):
+            for j in range(1, CHUNKS):
                 send_forecast(chip(k) + c, j)
-                return carry
-
-            lax.fori_loop(0, len(OFFSETS), send_rest, 0)
-            send_near(sibling, c, j)
-
-    lax.fori_loop(steps // 4, steps, select, 0, unroll=2)
-
-    def anomaly(r):
+            return inner
+
+        lax.fori_loop(0, CHIPS, send_rest, 0)
+        return carry
+
+    lax.fori_loop(0, 2, phase, 0)
+
+    lax.fori_loop(EARLY, steps, select, 0, unroll=2)
+
+    def anomaly(r, carry):
         v = region[:, r].astype(F32)
         for h in range(2):
             u = v[:, h * MD:(h + 1) * MD, :].reshape(M, BLK)
             u = u - jnp.sum(u, axis=0, keepdims=True) * (1.0 / M)
-            dev[:, r * Q + h * BLK:r * Q + (h + 1) * BLK] = u.astype(BF16)
-
-    for j, (row0, rows) in enumerate(CHUNKS):
-        arrived = region.at[:, pl.ds(row0, rows)]
+            dev[:, pl.ds(pl.multiple_of(r * Q + h * BLK, BLK), BLK)] = u.astype(BF16)
+        return carry
+
+    def lon_plan(src, dst, send_sem, recv_sem, t):
+        return pltpu.make_async_remote_copy(
+            src_ref=src, dst_ref=dst, send_sem=send_sem, recv_sem=recv_sem,
+            device_id={"lon": t}, device_id_type=MESH)
+
+    obs_halo = [
+        lon_plan(obs_all.at[pl.ds(CELLS, HALO)], obs_all.at[pl.ds(0, HALO)],
+                 oh_send.at[0], oh_recv.at[0], east),
+        lon_plan(obs_all.at[pl.ds(HALO, HALO)], obs_all.at[pl.ds(HALO + CELLS, HALO)],
+                 oh_send.at[1], oh_recv.at[1], west),
+    ]
+    obs_acc[...] = jnp.zeros((CELLS, M), F32)
+
+    def observe(j, carry):
+        arrived = region.at[:, pl.ds(j * PAIR, PAIR)]
         pltpu.make_async_copy(arrived, arrived, a_recv.at[j]).wait()
-        for r in range(row0, row0 + rows):
-            anomaly(r)
-        cells = slice(row0 * Q, (row0 + rows) * Q)
-
-        def product(o0, n, cells=cells):
-            return lax.dot_general(
-                sel[o0:o0 + n, cells], dev[:, cells],
-                (((1,), (1,)), ((), ())), preferred_element_type=F32)
-
-        if j == 0:
-            obs_acc[...] = product(0, CELLS)
-        elif j < len(CHUNKS) - 1:
-            obs_acc[...] += product(0, CELLS)
-        else:
-            for o0 in (0, CELLS - HALO):
-                total = obs_acc[o0:o0 + HALO, :] + product(o0, HALO)
-                obs_all[HALO + o0:HALO + o0 + HALO, :] = total.astype(BF16)
-            obs_halo = [
-                lon_copy(obs_all.at[pl.ds(CELLS, HALO)], obs_all.at[pl.ds(0, HALO)],
-                         oh_send.at[0], oh_recv.at[0], east),
-                lon_copy(obs_all.at[pl.ds(HALO, HALO)], obs_all.at[pl.ds(HALO + CELLS, HALO)],
-                         oh_send.at[1], oh_recv.at[1], west),
-            ]
-            total = obs_acc[HALO:CELLS - HALO, :] + product(HALO, CELLS - 2 * HALO)
-            obs_all[2 * HALO:CELLS, :] = total.astype(BF16)
+        lax.fori_loop(0, PAIR, lambda i, inner: anomaly(j * PAIR + i, inner), 0, unroll=2)
+        cells = pl.ds(pl.multiple_of(j * PAIR * Q, Q), PAIR * Q)
+
+        def product(k, inner):
+            o = jnp.where(k == 1, 3, jnp.where(k > 1, k - 1, 0))
+            at = pl.ds(pl.multiple_of(o * HALO, HALO), HALO)
+            total = obs_acc[at, :] + lax.dot_general(
+                sel[at, cells], dev[:, cells], (((1,), (1,)), ((), ())), preferred_element_type=F32)
+            obs_acc[at, :] = total
+            obs_all[pl.ds(pl.multiple_of(o * HALO + HALO, HALO), HALO), :] = total.astype(BF16)
+            return inner
+
+        lax.fori_loop(0, 2, product, 0)
+
+        @pl.when(j == CHUNKS - 1)
+        def _():
+            for copy in obs_halo:
+                copy.start()
+
+        lax.fori_loop(2, CELLS // HALO, product, 0)
+        return carry
+
+    lax.fori_loop(0, CHUNKS, observe, 0)
 
     to_scalar.wait()
 
     def covariance(r, candidates, tapered):
-        right = dev[:, pl.ds(pl.multiple_of(r * Q, Q), Q)]
+        right = dev[:, pl.ds(r * Q if isinstance(r, int) else pl.multiple_of(r * Q, Q), Q)]
         for n, i in enumerate(candidates):
             cov = jnp.dot(obs_all[i * Q:(i + 1) * Q, :], right, preferred_element_type=F32)
             for oh in range(2):
@@ -324,15 +343,11 @@
             change(2 * p, 0)
             cov(2 * p + 1, 1)
             change(2 * p + 1, 1)
-            cov(2 * p + 2, 0)
+            cov(jnp.minimum(2 * p + 2, ROWS - 1), 0)
             after(p)
             return carry
 
-        lax.fori_loop(0, ROWS // 2 - 1, step, 0)
-        change(ROWS - 2, 0)
-        cov(ROWS - 1, 1)
-        change(ROWS - 1, 1)
-        after(ROWS // 2 - 1)
+        lax.fori_loop(0, ROWS // 2, step, 0)
 
     own = (own0, own1)
 
@@ -355,6 +370,9 @@
         ]
         back[:, r] = jnp.concatenate(parts, axis=1).astype(BF16)
 
+    chip_columns = [lax.rem(my_x + offset, 4) * 2 for offset in (2, 1, 3, 0)]
+    sibling = lax.div(me, 2) * 2 + 1 - core
+
     def send_pair(p):
         rows = pl.ds(2 * p, 2)
 
@@ -365,19 +383,23 @@
                 device_id={"wide": other}, device_id_type=MESH).start()
 
         def send(k, carry):
-            other = chip(k)
-            send_back(other)
-            send_back(other + 1)
+            to_row = lax.rem(my_y + jnp.where(k == 0, 2, 2 * k - 1), 4) * 8
+            for column in chip_columns:
+                send_back(to_row + column)
+                send_back(to_row + column + 1)
             return carry
 
-        lax.fori_loop(0, len(OFFSETS), send, 0)
+        lax.fori_loop(0, 3, send, 0)
+        for column in chip_columns[:3]:
+            send_back(my_y * 8 + column)
+            send_back(my_y * 8 + column + 1)
         send_back(sibling)
         pltpu.make_async_copy(back.at[me, rows], home.at[me, rows], b_recv).start()
 
     pipelined(lambda r, slot: covariance(r, (0, 1, 10, 11), outer[slot]), outer_change, send_pair)
 
-    for j, (row0, rows) in enumerate(CHUNKS):
-        some = sent.at[pl.ds(0, NW - 1), pl.ds(row0, rows)]
+    for j in range(CHUNKS):
+        some = sent.at[pl.ds(0, NW - 1), pl.ds(j * PAIR, PAIR)]
         pltpu.make_async_copy(some, some, a_send.at[j]).wait()
     some = back.at[pl.ds(0, NW - 1)]
     pltpu.make_async_copy(some, some, b_send).wait()
@@ -407,10 +429,10 @@
         out_specs=anywhere,
         scratch_shapes=[
             pltpu.VMEM((MD, 256, Q), BF16),
-            pltpu.VMEM((MD, 256 + 16, Q), F32),
-            pltpu.VMEM((2, 32, BLK), BF16),
-            pltpu.VMEM((2, 32, BLK), BF16),
-            pltpu.VMEM((2, 32, BLK), F32),
+            pltpu.VMEM((256 + 2, MD, Q), F32),
+            pltpu.VMEM((2, 16, Q), BF16),
+            pltpu.VMEM((2, 16, Q), BF16),
+            pltpu.VMEM((2, 2, MD, BLK), F32),
             pltpu.VMEM((NW, ROWS, 16, BLK), BF16),
             pltpu.VMEM((NW, ROWS, 16, BLK), BF16),
             pltpu.VMEM((M, ROWS, Q), BF16),
@@ -434,13 +456,13 @@
             pltpu.VMEM((2 * HALO, Q), BF16),
             pltpu.VMEM((ROWS, M, Q), F32),
             pltpu.VMEM((NW, ROWS, 16, BLK), BF16),
-            dma((7,)), dma((2,)), dma((2,)), dma((len(CHUNKS),)), dma((len(CHUNKS),)),
+            dma((7,)), dma((2,)), dma((2,)), dma((CHUNKS,)), dma((CHUNKS,)),
             dma((2,)), dma((2,)), dma((2,)), dma((2,)), dma, dma, dma,
         ],
         compiler_params=pltpu.CompilerParams(
             collective_id=0, has_side_effects=True, vmem_limit_bytes=62 * 1024 * 1024),
     )(x, innov, obs_index, obs_weight, obs_list, tile_count, taper_class)
-    part = 8
+    part = NW // 2
     return pl.pallas_call(
         settle,
         out_shape=jax.ShapeDtypeStruct((MD, 256, Q), BF16),

time: 56.9 us -> 51.5 us (0.905)
  Pallas kernels: 56.7 us -> 51.4 us
    pallas_call x1, Pallas kernels: 53.1 us -> 49 us  [body(): pl.pallas_call(kernel, out_shape=jax.ShapeDtypeStruct((NW, ROWS, 16, BLK)...]
    pallas_call x1, Pallas kernels: 3.59 us -> 2.39 us  [body(): pl.pallas_call(settle, out_shape=jax.ShapeDtypeStruct((MD, 256, Q), BF16)...]
where the time goes in v3:
time: 51.5 us; the launch traced here: 51.4 us
  Pallas kernels  51.4 us (100%)
    pallas_call x1, Pallas kernels, body(): pl.pallas_call(kernel, out_shape=jax.ShapeDtypeStruct((NW, ROWS, 16, BLK)...  49 us
    pallas_call x1, Pallas kernels, body(): pl.pallas_call(settle, out_shape=jax.ShapeDtypeStruct((MD, 256, Q), BF16)...  2.39 us

profile of v3, /device:TPU:1, one launch (start us, length us, event | category | flops | bytes accessed | tf_op | source)
XLA Modules:
  0.0 51.4 jit_solution(17149509925387113448)
XLA Ops:
  0.0 49.0 %shard_map.73.home_ref = bf16[32,8,16,128]{3,2,1,0:T(8,128)(2,1)} custom-call(bf16[8,256,256]{2,1,0:T(8,128)(2,1)} %x_hbm.1, bf16[256,8,256]{2,1,0:T(8,128)(2,1)} %innov_hbm.1, s32[4,256,256]{2,1,0:T(8,128)} %idx_hbm.1, f32[4,256,256]{2,1,0:T(8,128)} %wgt_hbm.1, s32[1,16,16]{2,1,0:T(8,128)} %list_hbm.1, s32[1,16]{1,0:T(1,128)} %count_hbm.1, ...), custom_call_target="tpu_custom_call" | custom-call | tf_op jit(solution)/shard_map/pallas_call | solution.py:425
  49.0 2.4 %shard_map.74 = bf16[8,256,256]{2,1,0:T(8,128)(2,1)} custom-call(bf16[32,8,16,128]{3,2,1,0:T(8,128)(2,1)} %shard_map.73.home_ref), custom_call_target="tpu_custom_call" | custom-call | tf_op jit(solution)/shard_map/pallas_call | solution.py:466

commit v4 on v3

--- a/solution.py
+++ b/solution.py
@@ -23,8 +23,11 @@
 CAND = CELLS + 2 * HALO
 CHUNKS = 2
 PAIR = ROWS // CHUNKS
+PARTS = 4
+HALF = 4
 CHIPS = 16
-EARLY = 12
+STEP = 2
+EARLY = 6
 GROUP = 64
 
 
@@ -37,7 +40,7 @@
     x_in, x_f, edge_out, edge_in, edge_f, sent, region, innov_in, innov_all, idx, wgt, cols, sel,
     dev, obs_acc, obs_all, table, listed, classes, count_s, dense_v, dense_s,
     own0, own1, out0, out1, part, back,
-    load_sem, edge_send, edge_recv, a_send, a_recv, ih_send, ih_recv, oh_send, oh_recv,
+    x_sem, load_sem, edge_send, edge_recv, a_send, a_recv, ih_send, ih_recv, oh_send, oh_recv,
     b_send, b_recv, class_sem,
 ):
     me = lax.axis_index("wide")
@@ -59,7 +62,6 @@
     first = pl.multiple_of(me * ROWS, ROWS)
     loads = [
         pltpu.make_async_copy(src, dst, load_sem.at[i]) for i, (src, dst) in enumerate((
-            (x_hbm, x_in),
             (idx_hbm.at[:, pl.ds(first, ROWS), :], idx),
             (wgt_hbm.at[:, pl.ds(first, ROWS), :], wgt),
             (innov_hbm, innov_in),
@@ -68,9 +70,9 @@
             (class_hbm, classes),
         ))
     ]
-    load_x, load_idx, load_wgt, load_innov, load_list, load_count, load_class = loads
-    for load in loads:
-        load.start()
+    load_idx, load_wgt, load_innov, load_list, load_count, load_class = loads
+    load_x = pltpu.make_async_copy(x_hbm, x_in, x_sem)
+    load_x.start()
 
     barrier = pltpu.get_barrier_semaphore()
 
@@ -86,6 +88,8 @@
     x_f[0] = jnp.zeros((MD, Q), F32)
     x_f[257] = jnp.zeros((MD, Q), F32)
     load_x.wait()
+    for load in loads:
+        load.start()
 
     def widen(g, carry):
         r0 = pl.multiple_of(g * 16, 16)
@@ -112,28 +116,9 @@
         return place(firsts, carry[0]), place(lasts, carry[1])
 
     zeros = jnp.zeros((MD, Q), F32)
-    left, right = lax.fori_loop(0, 16, widen, (zeros, zeros), unroll=2)
+    left, right = lax.fori_loop(0, 16, widen, (zeros, zeros), unroll=4)
     edge_out[0] = jnp.concatenate([left, zeros], axis=0).astype(BF16)
     edge_out[1] = jnp.concatenate([right, zeros], axis=0).astype(BF16)
-
-    d = (iota((BLK, BLK), 0) - iota((BLK, BLK), 1)).astype(F32)
-    for c in range(4):
-        s = d * (1.0 / (8.0 * 2.0 ** c))
-        table[c] = (1.0 / (M - 1.0)) / (1.0 + s * s)
-    table[4] = jnp.zeros((BLK, BLK), F32)
-
-    load_idx.wait()
-    load_wgt.wait()
-    origin = me * CELLS
-
-    def columns(i, carry):
-        parts = [(idx[k, pl.ds(i, 1), :] - origin).astype(F32) for k in range(4)]
-        parts += [wgt[k, pl.ds(i, 1), :] for k in range(4)]
-        stacked = jnp.concatenate(parts + [jnp.zeros((BLK - 8, Q), F32)], axis=0)
-        cols[pl.ds(pl.multiple_of(i * Q, Q), Q), :] = jnp.transpose(stacked, (1, 0))
-        return carry
-
-    lax.fori_loop(0, ROWS, columns, 0, unroll=2)
 
     pl.semaphore_wait(barrier, NW - 1 + 2)
 
@@ -148,6 +133,19 @@
         lon_copy(edge_out.at[side], edge_in.at[side], edge_send.at[side], edge_recv.at[side], t)
         for side, t in ((0, west), (1, east))
     ]
+
+    load_idx.wait()
+    load_wgt.wait()
+    origin = me * CELLS
+
+    def columns(i, carry):
+        parts = [(idx[k, pl.ds(i, 1), :] - origin).astype(F32) for k in range(4)]
+        parts += [wgt[k, pl.ds(i, 1), :] for k in range(4)]
+        stacked = jnp.concatenate(parts + [jnp.zeros((BLK - 8, Q), F32)], axis=0)
+        cols[pl.ds(pl.multiple_of(i * Q, Q), Q), :] = jnp.transpose(stacked, (1, 0))
+        return carry
+
+    lax.fori_loop(0, ROWS, columns, 0, unroll=2)
 
     load_innov.wait()
 
@@ -167,6 +165,12 @@
         lon_copy(innov_all.at[:, pl.ds(HALO, HALO)], innov_all.at[:, pl.ds(HALO + CELLS, HALO)],
                  ih_send.at[1], ih_recv.at[1], west),
     ]
+
+    d = (iota((BLK, BLK), 0) - iota((BLK, BLK), 1)).astype(F32)
+    for c in range(4):
+        s = d * (1.0 / (8.0 * 2.0 ** c))
+        table[c] = (1.0 / (M - 1.0)) / (1.0 + s * s)
+    table[4] = jnp.zeros((BLK, BLK), F32)
 
     for load in (load_list, load_count, load_class):
         load.wait()
@@ -185,6 +189,7 @@
 
     def select(g, carry):
         o0 = pl.multiple_of(g * GROUP, GROUP)
+        to = pl.multiple_of(lax.rem(o0 + HALO, CELLS), GROUP)
         here = cols[pl.ds(o0, GROUP), :]
         cell = [jnp.broadcast_to(here[:, k:k + 1], (GROUP, BLK)) for k in range(4)]
         cell = [c.astype(jnp.int32).astype(jnp.int16) for c in cell]
@@ -202,7 +207,7 @@
             value = jnp.where(at == cell[0], sums[0], none)
             for k in range(1, 4):
                 value = jnp.where(at == cell[k], sums[k], value)
-            sel[pl.ds(o0, GROUP), t * BLK:(t + 1) * BLK] = value
+            sel[pl.ds(to, GROUP), t * BLK:(t + 1) * BLK] = value
         return carry
 
     steps = CELLS // GROUP
@@ -255,21 +260,21 @@
 
     def phase(c, carry):
         def compute_send(p, inner):
-            others = [chip(2 * p) + c, chip(2 * p + 1) + c]
+            others = [chip(STEP * p + i) + c for i in range(STEP)]
             for other in others:
                 forecast(other)
             for other in others:
                 send_forecast(other, 0)
             return inner
 
-        lax.fori_loop(0, CHIPS // 2, compute_send, 0)
+        lax.fori_loop(0, CHIPS // STEP, compute_send, 0)
 
         def send_rest(k, inner):
             for j in range(1, CHUNKS):
                 send_forecast(chip(k) + c, j)
             return inner
 
-        lax.fori_loop(0, CHIPS, send_rest, 0)
+        lax.fori_loop(0, CHIPS, send_rest, 0, unroll=4)
         return carry
 
     lax.fori_loop(0, 2, phase, 0)
@@ -297,32 +302,38 @@
     ]
     obs_acc[...] = jnp.zeros((CELLS, M), F32)
 
-    def observe(j, carry):
-        arrived = region.at[:, pl.ds(j * PAIR, PAIR)]
-        pltpu.make_async_copy(arrived, arrived, a_recv.at[j]).wait()
-        lax.fori_loop(0, PAIR, lambda i, inner: anomaly(j * PAIR + i, inner), 0, unroll=2)
+    def product(block, j):
+        at = pl.ds(pl.multiple_of(block * 2 * HALO, 2 * HALO), 2 * HALO)
         cells = pl.ds(pl.multiple_of(j * PAIR * Q, Q), PAIR * Q)
-
-        def product(k, inner):
-            o = jnp.where(k == 1, 3, jnp.where(k > 1, k - 1, 0))
-            at = pl.ds(pl.multiple_of(o * HALO, HALO), HALO)
-            total = obs_acc[at, :] + lax.dot_general(
-                sel[at, cells], dev[:, cells], (((1,), (1,)), ((), ())), preferred_element_type=F32)
-            obs_acc[at, :] = total
-            obs_all[pl.ds(pl.multiple_of(o * HALO + HALO, HALO), HALO), :] = total.astype(BF16)
-            return inner
-
-        lax.fori_loop(0, 2, product, 0)
-
-        @pl.when(j == CHUNKS - 1)
+        total = obs_acc[at, :] + lax.dot_general(
+            sel[at, cells], dev[:, cells], (((1,), (1,)), ((), ())), preferred_element_type=F32)
+        obs_acc[at, :] = total
+        some = total.astype(BF16)
+        to = pl.multiple_of(jnp.where(block == 0, CELLS, 2 * HALO), HALO)
+        obs_all[pl.ds(to, HALO), :] = some[:HALO]
+        to = pl.multiple_of(jnp.where(block == 0, HALO, 3 * HALO), HALO)
+        obs_all[pl.ds(to, HALO), :] = some[HALO:]
+
+    def observe(step, carry):
+        block = lax.div(step, CHUNKS)
+        j = lax.rem(step, CHUNKS)
+
+        @pl.when(block == 0)
+        def _():
+            arrived = region.at[:, pl.ds(j * PAIR, PAIR)]
+            pltpu.make_async_copy(arrived, arrived, a_recv.at[j]).wait()
+            lax.fori_loop(0, PAIR, lambda i, inner: anomaly(j * PAIR + i, inner), 0, unroll=2)
+
+        product(block, j)
+
+        @pl.when(step == CHUNKS - 1)
         def _():
             for copy in obs_halo:
                 copy.start()
 
-        lax.fori_loop(2, CELLS // HALO, product, 0)
-        return carry
-
-    lax.fori_loop(0, CHUNKS, observe, 0)
+        return carry
+
+    lax.fori_loop(0, 2 * CHUNKS, observe, 0)
 
     to_scalar.wait()
 
@@ -336,28 +347,23 @@
                     some = cov[oh * BLK:(oh + 1) * BLK, ch * BLK:(ch + 1) * BLK] * factor
                     tapered[n * Q + oh * BLK:n * Q + (oh + 1) * BLK, ch * BLK:(ch + 1) * BLK] = some.astype(BF16)
 
-    def pipelined(cov, change, after):
-        cov(0, 0)
-
+    def pipelined(base, cov, change, after):
         def step(p, carry):
-            change(2 * p, 0)
-            cov(2 * p + 1, 1)
-            change(2 * p + 1, 1)
-            cov(jnp.minimum(2 * p + 2, ROWS - 1), 0)
-            after(p)
+            r = base + 2 * p
+            change(r, 0)
+            cov(r + 1, 1)
+            change(r + 1, 1)
+            cov(jnp.minimum(r + 2, ROWS - 1), 0)
+            after(r)
             return carry
 
-        lax.fori_loop(0, ROWS // 2, step, 0)
+        lax.fori_loop(0, HALF // 2, step, 0)
 
     own = (own0, own1)
 
     def own_change(r, slot):
         part[r] = jnp.dot(innov_all[:, HALO:HALO + CELLS], own[slot][...], preferred_element_type=F32)
 
-    pipelined(lambda r, slot: covariance(r, range(2, 10), own[slot]), own_change, lambda p: None)
-
-    for copy in innov_halo + obs_halo:
-        copy.wait()
     outer = (out0, out1)
 
     def outer_change(r, slot):
@@ -373,8 +379,8 @@
     chip_columns = [lax.rem(my_x + offset, 4) * 2 for offset in (2, 1, 3, 0)]
     sibling = lax.div(me, 2) * 2 + 1 - core
 
-    def send_pair(p):
-        rows = pl.ds(2 * p, 2)
+    def send_pair(r):
+        rows = pl.ds(r, 2)
 
         def send_back(other):
             pltpu.make_async_remote_copy(
@@ -396,7 +402,28 @@
         send_back(sibling)
         pltpu.make_async_copy(back.at[me, rows], home.at[me, rows], b_recv).start()
 
-    pipelined(lambda r, slot: covariance(r, (0, 1, 10, 11), outer[slot]), outer_change, send_pair)
+    def own_covariance(r, slot):
+        covariance(r, range(2, 10), own[slot])
+
+    def outer_covariance(r, slot):
+        covariance(r, (0, 1, 10, 11), outer[slot])
+
+    own_covariance(0, 0)
+
+    def update(half, carry):
+        base = half * HALF
+        pipelined(base, own_covariance, own_change, lambda r: None)
+
+        @pl.when(half == 0)
+        def _():
+            for copy in innov_halo + obs_halo:
+                copy.wait()
+            outer_covariance(0, 0)
+
+        pipelined(base, outer_covariance, outer_change, send_pair)
+        return carry
+
+    lax.fori_loop(0, ROWS // HALF, update, 0)
 
     for j in range(CHUNKS):
         some = sent.at[pl.ds(0, NW - 1), pl.ds(j * PAIR, PAIR)]
@@ -406,17 +433,36 @@
     pltpu.make_async_copy(home, home, b_recv).wait()
 
 
-def settle(home_ref, out_ref):
+def settle(home, out, home_in, out_v, in_sem, out_sem):
+    regions = NW // PARTS
+    loads = [
+        pltpu.make_async_copy(home.at[pl.ds(i * regions, regions)], home_in.at[pl.ds(i * regions, regions)], in_sem.at[i])
+        for i in range(PARTS)
+    ]
+    stores = [
+        pltpu.make_async_copy(
+            out_v.at[:, pl.ds(i * regions * ROWS, regions * ROWS)],
+            out.at[:, pl.ds(i * regions * ROWS, regions * ROWS)], out_sem.at[i])
+        for i in range(PARTS)
+    ]
+    for load in loads:
+        load.start()
+
     def pair(g, carry):
-        v = home_ref[pl.ds(2 * g, 2)].astype(F32)
+        v = home_in[pl.ds(2 * g, 2)].astype(F32)
         for h in range(2):
             u = v[:, :, h * MD:(h + 1) * MD, :]
             parts = [jnp.transpose(u[0], (1, 0, 2)), jnp.transpose(u[1], (1, 0, 2))]
-            out_ref[:, pl.ds(pl.multiple_of(g * 16, 16), 16), h * BLK:(h + 1) * BLK] = (
+            out_v[:, pl.ds(pl.multiple_of(g * 16, 16), 16), h * BLK:(h + 1) * BLK] = (
                 jnp.concatenate(parts, axis=1).astype(BF16))
         return carry
 
-    lax.fori_loop(0, home_ref.shape[0] // 2, pair, 0, unroll=2)
+    for i in range(PARTS):
+        loads[i].wait()
+        lax.fori_loop(i * regions // 2, (i + 1) * regions // 2, pair, 0, unroll=2)
+        stores[i].start()
+    for store in stores:
+        store.wait()
 
 
 def body(x, innov, obs_index, obs_weight, obs_list, tile_count, taper_class):
@@ -456,19 +502,23 @@
             pltpu.VMEM((2 * HALO, Q), BF16),
             pltpu.VMEM((ROWS, M, Q), F32),
             pltpu.VMEM((NW, ROWS, 16, BLK), BF16),
-            dma((7,)), dma((2,)), dma((2,)), dma((CHUNKS,)), dma((CHUNKS,)),
+            dma, dma((6,)), dma((2,)), dma((2,)), dma((CHUNKS,)), dma((CHUNKS,)),
             dma((2,)), dma((2,)), dma((2,)), dma((2,)), dma, dma, dma,
         ],
         compiler_params=pltpu.CompilerParams(
             collective_id=0, has_side_effects=True, vmem_limit_bytes=62 * 1024 * 1024),
     )(x, innov, obs_index, obs_weight, obs_list, tile_count, taper_class)
-    part = NW // 2
     return pl.pallas_call(
         settle,
         out_shape=jax.ShapeDtypeStruct((MD, 256, Q), BF16),
-        grid=(NW // part,),
-        in_specs=[pl.BlockSpec((part, ROWS, 16, BLK), lambda i: (i, 0, 0, 0))],
-        out_specs=pl.BlockSpec((MD, part * ROWS, Q), lambda i: (0, i, 0)),
+        in_specs=[anywhere],
+        out_specs=anywhere,
+        scratch_shapes=[
+            pltpu.VMEM((NW, ROWS, 16, BLK), BF16),
+            pltpu.VMEM((MD, 256, Q), BF16),
+            dma((PARTS,)), dma((PARTS,)),
+        ],
+        compiler_params=pltpu.CompilerParams(vmem_limit_bytes=62 * 1024 * 1024),
     )(home)
 
 

time: 51.5 us -> 50.8 us (0.986)
  Pallas kernels: 51.4 us -> 50.7 us
    pallas_call x1, Pallas kernels: 49 us -> 48.4 us  [body(): pl.pallas_call(kernel, out_shape=jax.ShapeDtypeStruct((NW, ROWS, 16, BLK)...]
where the time goes in v4:
time: 50.8 us; the launch traced here: 50.7 us
  Pallas kernels  50.7 us (100%)
    pallas_call x1, Pallas kernels, body(): pl.pallas_call(kernel, out_shape=jax.ShapeDtypeStruct((NW, ROWS, 16, BLK)...  48.4 us
    pallas_call x1, Pallas kernels, body(): pl.pallas_call(settle, out_shape=jax.ShapeDtypeStruct((MD, 256, Q), BF16)...  2.24 us

profile of v4, /device:TPU:1, one launch (start us, length us, event | category | flops | bytes accessed | tf_op | source)
XLA Modules:
  0.0 50.7 jit_solution(17869585911009977072)
XLA Ops:
  0.0 48.4 %shard_map.73.home = bf16[32,8,16,128]{3,2,1,0:T(8,128)(2,1)} custom-call(bf16[8,256,256]{2,1,0:T(8,128)(2,1)} %x_hbm.1, bf16[256,8,256]{2,1,0:T(8,128)(2,1)} %innov_hbm.1, s32[4,256,256]{2,1,0:T(8,128)} %idx_hbm.1, f32[4,256,256]{2,1,0:T(8,128)} %wgt_hbm.1, s32[1,16,16]{2,1,0:T(8,128)} %list_hbm.1, s32[1,16]{1,0:T(1,128)} %count_hbm.1, s32[1,16,16]{2,1,0:T(8,128)} %class_hbm.1), custom_call_target="tpu_custom_call" | custom-call | tf_op jit(solution)/shard_map/pallas_call | solution.py:471
  48.4 2.2 %shard_map.74 = bf16[8,256,256]{2,1,0:T(8,128)(2,1)} custom-call(bf16[32,8,16,128]{3,2,1,0:T(8,128)(2,1)} %shard_map.73.home), custom_call_target="tpu_custom_call" | custom-call | tf_op jit(solution)/shard_map/pallas_call | solution.py:511

commit v5 on v4

--- a/solution.py
+++ b/solution.py
@@ -24,7 +24,7 @@
 CHUNKS = 2
 PAIR = ROWS // CHUNKS
 PARTS = 4
-HALF = 4
+FIRST = 2
 CHIPS = 16
 STEP = 2
 EARLY = 6
@@ -138,14 +138,11 @@
     load_wgt.wait()
     origin = me * CELLS
 
-    def columns(i, carry):
-        parts = [(idx[k, pl.ds(i, 1), :] - origin).astype(F32) for k in range(4)]
-        parts += [wgt[k, pl.ds(i, 1), :] for k in range(4)]
-        stacked = jnp.concatenate(parts + [jnp.zeros((BLK - 8, Q), F32)], axis=0)
-        cols[pl.ds(pl.multiple_of(i * Q, Q), Q), :] = jnp.transpose(stacked, (1, 0))
-        return carry
-
-    lax.fori_loop(0, ROWS, columns, 0, unroll=2)
+    entries = [(idx[k] - origin).astype(F32) for k in range(4)] + [wgt[k] for k in range(4)]
+    entries = jnp.concatenate(entries + [jnp.zeros((BLK - 8 * ROWS, Q), F32)], axis=0)
+    entries = jnp.transpose(entries, (1, 0))
+    for i in range(ROWS):
+        cols[i * Q:(i + 1) * Q, :] = pltpu.roll(entries, BLK - i, 1) if i else entries
 
     load_innov.wait()
 
@@ -191,9 +188,9 @@
         o0 = pl.multiple_of(g * GROUP, GROUP)
         to = pl.multiple_of(lax.rem(o0 + HALO, CELLS), GROUP)
         here = cols[pl.ds(o0, GROUP), :]
-        cell = [jnp.broadcast_to(here[:, k:k + 1], (GROUP, BLK)) for k in range(4)]
+        cell = [jnp.broadcast_to(here[:, 8 * k:8 * k + 1], (GROUP, BLK)) for k in range(4)]
         cell = [c.astype(jnp.int32).astype(jnp.int16) for c in cell]
-        weight = [jnp.broadcast_to(here[:, 4 + k:5 + k], (GROUP, BLK)).astype(BF16) for k in range(4)]
+        weight = [jnp.broadcast_to(here[:, 32 + 8 * k:33 + 8 * k], (GROUP, BLK)).astype(BF16) for k in range(4)]
         none = jnp.zeros((GROUP, BLK), BF16)
         sums = []
         for k in range(4):
@@ -240,8 +237,7 @@
             halves = []
             for h, (c, e, w) in enumerate(((a, e_a, w_a), (b, e_b, w_b))):
                 hs = slice(h * BLK, (h + 1) * BLK)
-                spread = e + w + n[:, hs] + s[:, hs] - 4.0 * c
-                halves.append(c + 0.2 * spread - 0.3 * (e - w))
+                halves.append(0.2 * (c + (n[:, hs] + s[:, hs])) + (0.5 * w - 0.1 * e))
             sent[r, i] = jnp.concatenate(halves, axis=0).astype(BF16)
 
     def send_forecast(other, j):
@@ -347,9 +343,9 @@
                     some = cov[oh * BLK:(oh + 1) * BLK, ch * BLK:(ch + 1) * BLK] * factor
                     tapered[n * Q + oh * BLK:n * Q + (oh + 1) * BLK, ch * BLK:(ch + 1) * BLK] = some.astype(BF16)
 
-    def pipelined(base, cov, change, after):
+    def pipelined(pairs, cov, change, after):
         def step(p, carry):
-            r = base + 2 * p
+            r = 2 * p
             change(r, 0)
             cov(r + 1, 1)
             change(r + 1, 1)
@@ -357,7 +353,7 @@
             after(r)
             return carry
 
-        lax.fori_loop(0, HALF // 2, step, 0)
+        lax.fori_loop(*pairs, step, 0)
 
     own = (own0, own1)
 
@@ -410,20 +406,20 @@
 
     own_covariance(0, 0)
 
-    def update(half, carry):
-        base = half * HALF
-        pipelined(base, own_covariance, own_change, lambda r: None)
-
-        @pl.when(half == 0)
+    def update(late, carry):
+        pairs = (late * FIRST, FIRST + late * (ROWS // 2 - FIRST))
+        pipelined(pairs, own_covariance, own_change, lambda r: None)
+
+        @pl.when(late == 0)
         def _():
             for copy in innov_halo + obs_halo:
                 copy.wait()
             outer_covariance(0, 0)
 
-        pipelined(base, outer_covariance, outer_change, send_pair)
-        return carry
-
-    lax.fori_loop(0, ROWS // HALF, update, 0)
+        pipelined(pairs, outer_covariance, outer_change, send_pair)
+        return carry
+
+    lax.fori_loop(0, 2, update, 0)
 
     for j in range(CHUNKS):
         some = sent.at[pl.ds(0, NW - 1), pl.ds(j * PAIR, PAIR)]

time: 50.8 us -> 49.6 us (0.976)
  Pallas kernels: 50.7 us -> 49.5 us
    pallas_call x1, Pallas kernels: 48.4 us -> 47.2 us  [body(): pl.pallas_call(kernel, out_shape=jax.ShapeDtypeStruct((NW, ROWS, 16, BLK)...]
where the time goes in v5:
time: 49.6 us; the launch traced here: 49.5 us
  Pallas kernels  49.5 us (100%)
    pallas_call x1, Pallas kernels, body(): pl.pallas_call(kernel, out_shape=jax.ShapeDtypeStruct((NW, ROWS, 16, BLK)...  47.2 us
    pallas_call x1, Pallas kernels, body(): pl.pallas_call(settle, out_shape=jax.ShapeDtypeStruct((MD, 256, Q), BF16)...  2.24 us

profile of v5, /device:TPU:1, one launch (start us, length us, event | category | flops | bytes accessed | tf_op | source)
XLA Modules:
  0.0 49.5 jit_solution(12003678655974357038)
XLA Ops:
  0.0 47.2 %shard_map.73.home = bf16[32,8,16,128]{3,2,1,0:T(8,128)(2,1)} custom-call(bf16[8,256,256]{2,1,0:T(8,128)(2,1)} %x_hbm.1, bf16[256,8,256]{2,1,0:T(8,128)(2,1)} %innov_hbm.1, s32[4,256,256]{2,1,0:T(8,128)} %idx_hbm.1, f32[4,256,256]{2,1,0:T(8,128)} %wgt_hbm.1, s32[1,16,16]{2,1,0:T(8,128)} %list_hbm.1, s32[1,16]{1,0:T(1,128)} %count_hbm.1, s32[1,16,16]{2,1,0:T(8,128)} %class_hbm.1), custom_call_target="tpu_custom_call" | custom-call | tf_op jit(solution)/shard_map/pallas_call | solution.py:467
  47.2 2.2 %shard_map.74 = bf16[8,256,256]{2,1,0:T(8,128)(2,1)} custom-call(bf16[32,8,16,128]{3,2,1,0:T(8,128)(2,1)} %shard_map.73.home), custom_call_target="tpu_custom_call" | custom-call | tf_op jit(solution)/shard_map/pallas_call | solution.py:507
